TPU v7x, 32 devices: a whole 2x2x4 slice. The times are simulated.
32 devices in a mesh: dp: 2 (over x), mp: 4 (over y, core), width: 4 (over z).
Axes of the slice: x: 2, y: 2, z: 4, core: 2. Of those that a mesh axis runs over, the one named last changes fastest.
Arguments:
- tokens: bfloat16 [16, 1024, 512], P(('dp', 'width'), 'mp'), may hold values from -6 to 6
- segments: int32 [16, 1024], P(('dp', 'width')), may hold values from -1 to 7, as said below
- cotangent: bfloat16 [16, 1024, 512], P(('dp', 'width'), 'mp'), may hold values from -6 to 6
- norm_gains: bfloat16 [2, 2, 512], P(None, None, ('dp', 'width')), may hold values from 0.5 to 1.5
- biases: bfloat16 [2, 4, 512], P(None, None, ('dp', 'width')), may hold values from -3 to 3
- w_qkv: bfloat16 [2, 512, 3, 512], P(None, ('dp', 'width'), None, 'mp'), may hold values from -0.375 to 0.375
- w_out: bfloat16 [2, 512, 512], P(None, 'mp', ('dp', 'width')), may hold values from -3 to 3
- w_gate: bfloat16 [2, 2, 512, 512], P(None, None, ('dp', 'width'), 'mp'), may hold values from -0.25 to 0.25
- w_up: bfloat16 [2, 512, 2048], P(None, ('dp', 'width'), 'mp'), may hold values from -0.25 to 0.25
- w_down: bfloat16 [2, 2048, 512], P(None, 'mp', ('dp', 'width')), may hold values from -0.125 to 0.125
Outputs:
- output: float32 [16, 1024, 512], P(('dp', 'width'), 'mp')
- d_tokens: float32 [16, 1024, 512], P(('dp', 'width'), 'mp')
- d_norm_gains: float32 [2, 2, 512], P(None, None, ('dp', 'width'))
- d_norm_biases: float32 [2, 2, 512], P(None, None, ('dp', 'width'))
- d_gate_biases: float32 [2, 2, 512], P(None, None, ('dp', 'width'))
- d_w_qkv: float32 [2, 512, 3, 512], P(None, ('dp', 'width'), None, 'mp')
- d_w_out: float32 [2, 512, 512], P(None, 'mp', ('dp', 'width'))
- d_w_gate: float32 [2, 2, 512, 512], P(None, None, ('dp', 'width'), 'mp')
- d_w_up: float32 [2, 512, 2048], P(None, ('dp', 'width'), 'mp')
- d_w_down: float32 [2, 2048, 512], P(None, 'mp', ('dp', 'width'))
Inputs may be any that keep to these rules, and one draw needn't show every extreme that they name: `segments`: ids never fall along a packed row; -1 marks padding, which fills the end of a row. Of the 2 rows of one index of dp and width, one, chosen by the seed, is a single sequence of 1024 positions; every other row holds sequences 0 to 7, each of 32 to 64 positions, then padding.
All inputs are finite; a program needn't handle non-finite values.
Results may differ from a plain program's by a relative error of at most 0.025.
Values may be sent and summed in bfloat16 or wider, within the bound.
No kernel may reach another device: no remote copies, remote signals or barrier semaphores. Data moves between devices by JAX's collectives and lax.ppermute only.
A program may use at most 192 MiB of HBM per device.

v0:
```python
import jax
import jax.numpy as jnp
from jax import lax
from jax.sharding import PartitionSpec as P

HEAD_DIM = 64


norm_eps = 1e-05


def layer_norm(values, gain_row, bias_row):
    mean_val = jnp.mean(values, axis=-1, keepdims=True)
    centred = values - mean_val
    spread = jnp.mean(centred * centred, axis=-1, keepdims=True)
    return centred * lax.rsqrt(spread + norm_eps) * gain_row + bias_row


def gelu_tanh(values):
    return jax.nn.gelu(values, approximate=True)


def norm_rows(values, gain_row, bias_row):
    return layer_norm(values, gain_row.astype(jnp.float32), bias_row.astype(jnp.float32))


def spread_rows(rows_bf):
    return lax.all_gather(rows_bf, "mp", axis=0, tiled=True)


def collect_rows(branch_term):
    return lax.psum_scatter(
        branch_term.astype(jnp.bfloat16), "mp", scatter_dimension=0, tiled=True
    ).astype(jnp.float32)


def spread_grads(rows_bf):
    return lax.all_gather(rows_bf, "mp", axis=0, tiled=True)


def collect_grads(branch_term):
    return lax.psum_scatter(
        branch_term.astype(jnp.bfloat16), "mp", scatter_dimension=0, tiled=True
    ).astype(jnp.float32)


def add_columns(branch_term, piece_cols, col_start):
    current = lax.dynamic_slice_in_dim(branch_term, col_start, piece_cols.shape[1], 1)
    return lax.dynamic_update_slice_in_dim(branch_term, current + piece_cols, col_start, 1)


def dot_plain(left_mat, right_mat):
    return jnp.dot(left_mat, right_mat, preferred_element_type=jnp.float32)


def dot_left_t(left_mat, right_mat):
    return lax.dot_general(
        left_mat, right_mat, (((0,), (0,)), ((), ())), preferred_element_type=jnp.float32
    )


def dot_right_t(left_mat, right_mat):
    return lax.dot_general(
        left_mat, right_mat, (((1,), (1,)), ((), ())), preferred_element_type=jnp.float32
    )


def allowed_span(seg_row, offset, span_rows):
    query_seg = seg_row[offset : offset + span_rows]
    query_pos = offset + jnp.arange(span_rows)
    key_pos = jnp.arange(seg_row.shape[0])
    return (query_seg[:, None] == seg_row[None, :]) & (key_pos[None, :] <= query_pos[:, None])


def split_heads(mixed_qkv):
    length = mixed_qkv.shape[0]
    return mixed_qkv.reshape(length, 3, mixed_qkv.shape[1] // (3 * HEAD_DIM), HEAD_DIM)


def attend(mixed_qkv, seg_row):
    head_parts = split_heads(mixed_qkv)
    queries, key_rows, value_rows = (head_parts[:, 0], head_parts[:, 1], head_parts[:, 2])
    length = mixed_qkv.shape[0]
    span_rows = min(512, length)
    score_scale = HEAD_DIM ** (-0.5)
    outputs = []
    log_sums = []
    for offset in range(0, length, span_rows):
        scores = (
            jnp.einsum(
                "qhd,khd->hqk",
                queries[offset : offset + span_rows],
                key_rows,
                preferred_element_type=jnp.float32,
            )
            * score_scale
        )
        scores = jnp.where(allowed_span(seg_row, offset, span_rows)[None], scores, -1e30)
        top_score = jnp.max(scores, axis=-1, keepdims=True)
        exp_scores = jnp.exp(scores - top_score)
        totals = jnp.sum(exp_scores, axis=-1, keepdims=True)
        probs_bf = (exp_scores / totals).astype(jnp.bfloat16)
        outputs.append(
            jnp.einsum("hqk,khd->qhd", probs_bf, value_rows, preferred_element_type=jnp.float32)
        )
        log_sums.append(top_score + jnp.log(totals))
    attended = jnp.concatenate(outputs, axis=0).reshape(length, -1).astype(jnp.bfloat16)
    return (attended, jnp.concatenate(log_sums, axis=1))


def attend_back(mixed_qkv, seg_row, log_sums, grad_att):
    head_parts = split_heads(mixed_qkv)
    queries, key_rows, value_rows = (head_parts[:, 0], head_parts[:, 1], head_parts[:, 2])
    length = mixed_qkv.shape[0]
    heads_here = head_parts.shape[2]
    grad_heads = grad_att.reshape(length, heads_here, HEAD_DIM)
    span_rows = min(512, length)
    score_scale = HEAD_DIM ** (-0.5)
    grad_query = []
    grad_key = jnp.zeros((length, heads_here, HEAD_DIM), jnp.float32)
    grad_value = jnp.zeros((length, heads_here, HEAD_DIM), jnp.float32)
    for offset in range(0, length, span_rows):
        query_span = queries[offset : offset + span_rows]
        grad_span = grad_heads[offset : offset + span_rows]
        scores = (
            jnp.einsum("qhd,khd->hqk", query_span, key_rows, preferred_element_type=jnp.float32)
            * score_scale
        )
        scores = jnp.where(allowed_span(seg_row, offset, span_rows)[None], scores, -1e30)
        probs_f = jnp.exp(scores - log_sums[:, offset : offset + span_rows])
        grad_value = grad_value + jnp.einsum(
            "hqk,qhd->khd",
            probs_f.astype(jnp.bfloat16),
            grad_span,
            preferred_element_type=jnp.float32,
        )
        grad_probs = jnp.einsum(
            "qhd,khd->hqk", grad_span, value_rows, preferred_element_type=jnp.float32
        )
        delta_row = jnp.sum(probs_f * grad_probs, axis=-1, keepdims=True)
        grad_scores = (probs_f * (grad_probs - delta_row)).astype(jnp.bfloat16)
        grad_query.append(
            jnp.einsum("hqk,khd->qhd", grad_scores, key_rows, preferred_element_type=jnp.float32)
            * score_scale
        )
        grad_key = (
            grad_key
            + jnp.einsum(
                "hqk,qhd->khd", grad_scores, query_span, preferred_element_type=jnp.float32
            )
            * score_scale
        )
    stacked = jnp.stack([jnp.concatenate(grad_query, axis=0), grad_key, grad_value], axis=1)
    return stacked.reshape(length, -1).astype(jnp.bfloat16)


def layer_forward(residual, seg_row, copies, col_start):
    gain_rows, bias_rows, qkv_w, out_w, gate_w, up_w, down_w = copies
    col_count = out_w.shape[0]
    gate_bias = lax.dynamic_slice_in_dim(bias_rows, col_start, col_count, 1).astype(jnp.float32)
    normed = spread_rows(norm_rows(residual, gain_rows[0], bias_rows[0]).astype(jnp.bfloat16))
    mixed_qkv = dot_plain(normed, qkv_w.reshape(qkv_w.shape[0], -1)).astype(jnp.bfloat16)
    attended, log_sums = attend(mixed_qkv, seg_row)
    gate_one = jax.nn.sigmoid(dot_plain(normed, gate_w[0]) + gate_bias[1])
    normed_cols = lax.dynamic_slice_in_dim(normed, col_start, col_count, 1).astype(jnp.float32)
    branch_term = add_columns(dot_plain(attended, out_w), gate_one * normed_cols, col_start)
    middle = residual + collect_rows(branch_term)
    normed_two = spread_rows(norm_rows(middle, gain_rows[1], bias_rows[2]).astype(jnp.bfloat16))
    hidden = dot_plain(normed_two, up_w)
    active = gelu_tanh(hidden).astype(jnp.bfloat16)
    gate_two = jax.nn.sigmoid(dot_plain(normed_two, gate_w[1]) + gate_bias[3])
    normed_two_cols = lax.dynamic_slice_in_dim(normed_two, col_start, col_count, 1).astype(
        jnp.float32
    )
    branch_term = add_columns(dot_plain(active, down_w), gate_two * normed_two_cols, col_start)
    result = middle + collect_rows(branch_term)
    kept_rows = (
        residual,
        normed,
        mixed_qkv,
        attended,
        log_sums,
        gate_one,
        middle,
        normed_two,
        hidden,
        active,
        gate_two,
    )
    return (result, kept_rows)


def layer_backward(grad_out, seg_row, copies, kept_rows, col_start):
    gain_rows, bias_rows, qkv_w, out_w, gate_w, up_w, down_w = copies
    (
        residual,
        normed,
        mixed_qkv,
        attended,
        log_sums,
        gate_one,
        middle,
        normed_two,
        hidden,
        active,
        gate_two,
    ) = kept_rows
    col_count = out_w.shape[0]
    width_all = normed.shape[1]
    branch_two = spread_grads(grad_out.astype(jnp.bfloat16))
    grad_down = dot_left_t(active, branch_two)
    grad_active = dot_right_t(branch_two, down_w)
    gelu_pull = jax.vjp(gelu_tanh, hidden)[1]
    grad_hidden = gelu_pull(grad_active)[0].astype(jnp.bfloat16)
    branch_cols = lax.dynamic_slice_in_dim(branch_two, col_start, col_count, 1).astype(jnp.float32)
    normed_two_cols = lax.dynamic_slice_in_dim(normed_two, col_start, col_count, 1).astype(
        jnp.float32
    )
    grad_gate_two = (branch_cols * normed_two_cols * gate_two * (1.0 - gate_two)).astype(
        jnp.bfloat16
    )
    grad_normed_two = dot_right_t(grad_hidden, up_w) + dot_right_t(grad_gate_two, gate_w[1])
    grad_normed_two = add_columns(grad_normed_two, branch_cols * gate_two, col_start)
    grad_up = dot_left_t(normed_two, grad_hidden)
    grad_gate_two_w = dot_left_t(normed_two, grad_gate_two)
    bias_gate_two = jnp.sum(grad_gate_two.astype(jnp.float32), axis=0)
    grad_rows_two = collect_grads(grad_normed_two)
    norm_pull = jax.vjp(
        layer_norm, middle, gain_rows[1].astype(jnp.float32), bias_rows[2].astype(jnp.float32)
    )[1]
    grad_mid_in, grad_gain_two, grad_bias_two = norm_pull(grad_rows_two)
    grad_middle = grad_out + grad_mid_in
    branch_one = spread_grads(grad_middle.astype(jnp.bfloat16))
    grad_out_w = dot_left_t(attended, branch_one)
    grad_att = dot_right_t(branch_one, out_w).astype(jnp.bfloat16)
    grad_mixed = attend_back(mixed_qkv, seg_row, log_sums, grad_att)
    branch_cols = lax.dynamic_slice_in_dim(branch_one, col_start, col_count, 1).astype(jnp.float32)
    normed_cols = lax.dynamic_slice_in_dim(normed, col_start, col_count, 1).astype(jnp.float32)
    grad_gate_one = (branch_cols * normed_cols * gate_one * (1.0 - gate_one)).astype(jnp.bfloat16)
    flat_qkv = qkv_w.reshape(qkv_w.shape[0], -1)
    grad_normed = dot_right_t(grad_mixed, flat_qkv) + dot_right_t(grad_gate_one, gate_w[0])
    grad_normed = add_columns(grad_normed, branch_cols * gate_one, col_start)
    grad_qkv = dot_left_t(normed, grad_mixed).reshape(qkv_w.shape)
    grad_gate_one_w = dot_left_t(normed, grad_gate_one)
    bias_gate_one = jnp.sum(grad_gate_one.astype(jnp.float32), axis=0)
    grad_rows_one = collect_grads(grad_normed)
    norm_pull = jax.vjp(
        layer_norm, residual, gain_rows[0].astype(jnp.float32), bias_rows[0].astype(jnp.float32)
    )[1]
    grad_in, grad_gain_one, grad_bias_one = norm_pull(grad_rows_one)
    grad_residual = grad_middle + grad_in
    zeros_row = jnp.zeros((width_all,), jnp.float32)
    grad_gains = jnp.stack([grad_gain_one, grad_gain_two])
    grad_biases = jnp.stack(
        [
            grad_bias_one,
            lax.dynamic_update_slice_in_dim(zeros_row, bias_gate_one, col_start, 0),
            grad_bias_two,
            lax.dynamic_update_slice_in_dim(zeros_row, bias_gate_two, col_start, 0),
        ]
    )
    grad_terms = (
        grad_gains,
        grad_biases,
        grad_qkv,
        grad_out_w,
        jnp.stack([grad_gate_one_w, grad_gate_two_w]),
        grad_up,
        grad_down,
    )
    return (grad_residual, grad_terms)


def add_tree(prior_sum, new_sum):
    if prior_sum is None:
        return new_sum
    return jax.tree.map(jnp.add, prior_sum, new_sum)


def on_device(tokens, segments, cotangent, norm_gains, biases, w_qkv, w_out, w_gate, w_up, w_down):
    batch_count = tokens.shape[0]
    part_rows = tokens.shape[1]
    layer_count = w_qkv.shape[0]
    col_start = lax.axis_index("mp") * w_out.shape[1]

    def copy_layer(layer_index):
        return (
            lax.all_gather(norm_gains[layer_index], ("dp", "width"), axis=1, tiled=True),
            lax.all_gather(biases[layer_index], ("dp", "width"), axis=1, tiled=True),
            lax.all_gather(w_qkv[layer_index], ("dp", "width"), axis=0, tiled=True),
            lax.all_gather(w_out[layer_index], ("dp", "width"), axis=1, tiled=True),
            lax.all_gather(w_gate[layer_index], ("dp", "width"), axis=1, tiled=True),
            lax.all_gather(w_up[layer_index], ("dp", "width"), axis=0, tiled=True),
            lax.all_gather(w_down[layer_index], ("dp", "width"), axis=1, tiled=True),
        )

    shard_sums = [None] * layer_count
    outputs = []
    grad_tokens = []
    for batch_index in range(batch_count):
        seg_row = segments[batch_index]
        residual = tokens[batch_index].astype(jnp.float32)
        saved_rows = []
        for layer_index in range(layer_count):
            copies = copy_layer(layer_index)
            residual, kept_rows = layer_forward(residual, seg_row, copies, col_start)
            saved_rows.append(kept_rows)
        outputs.append(residual)
        own_seg = lax.dynamic_slice_in_dim(seg_row, lax.axis_index("mp") * part_rows, part_rows, 0)
        grad_residual = (
            cotangent[batch_index].astype(jnp.float32) * (own_seg >= 0).astype(jnp.float32)[:, None]
        )
        for layer_index in reversed(range(layer_count)):
            copies = copy_layer(layer_index)
            grad_residual, grad_terms = layer_backward(
                grad_residual, seg_row, copies, saved_rows[layer_index], col_start
            )
            shard_sums[layer_index] = add_tree(
                shard_sums[layer_index],
                (
                    lax.psum_scatter(
                        grad_terms[0], ("dp", "width"), scatter_dimension=1, tiled=True
                    ),
                    lax.psum_scatter(
                        grad_terms[1], ("dp", "width"), scatter_dimension=1, tiled=True
                    ),
                    lax.psum_scatter(
                        grad_terms[2], ("dp", "width"), scatter_dimension=0, tiled=True
                    ),
                    lax.psum_scatter(
                        grad_terms[3], ("dp", "width"), scatter_dimension=1, tiled=True
                    ),
                    lax.psum_scatter(
                        grad_terms[4], ("dp", "width"), scatter_dimension=1, tiled=True
                    ),
                    lax.psum_scatter(
                        grad_terms[5], ("dp", "width"), scatter_dimension=0, tiled=True
                    ),
                    lax.psum_scatter(
                        grad_terms[6], ("dp", "width"), scatter_dimension=1, tiled=True
                    ),
                ),
            )
        grad_tokens.append(grad_residual)
    stacked_grads = [
        jnp.stack([shard_sums[layer_index][member] for layer_index in range(layer_count)])
        for member in range(7)
    ]
    gain_total, bias_total = lax.psum((stacked_grads[0], stacked_grads[1]), "mp")
    return (
        jnp.stack(outputs),
        jnp.stack(grad_tokens),
        gain_total,
        bias_total[:, 0::2],
        bias_total[:, 1::2],
        stacked_grads[2],
        stacked_grads[3],
        stacked_grads[4],
        stacked_grads[5],
        stacked_grads[6],
    )


def solution(mesh):
    placed = (
        P(("dp", "width"), "mp", None),
        P(("dp", "width"), None),
        P(("dp", "width"), "mp", None),
        P(None, None, ("dp", "width")),
        P(None, None, ("dp", "width")),
        P(None, ("dp", "width"), None, "mp"),
        P(None, "mp", ("dp", "width")),
        P(None, None, ("dp", "width"), "mp"),
        P(None, ("dp", "width"), "mp"),
        P(None, "mp", ("dp", "width")),
    )
    return jax.shard_map(
        on_device,
        mesh=mesh,
        in_specs=placed,
        out_specs=(
            P(("dp", "width"), "mp", None),
            P(("dp", "width"), "mp", None),
            P(None, None, ("dp", "width")),
            P(None, None, ("dp", "width")),
            P(None, None, ("dp", "width")),
            P(None, ("dp", "width"), None, "mp"),
            P(None, "mp", ("dp", "width")),
            P(None, None, ("dp", "width"), "mp"),
            P(None, ("dp", "width"), "mp"),
            P(None, "mp", ("dp", "width")),
        ),
        check_vma=False,
    )
```

profile of v0, /device:TPU:0, one launch (start us, length us, event | category | flops | bytes accessed | tf_op | source)
XLA Modules:
  0.0 2104.6 jit_solution(8611381537400471870)
XLA Ops:
  11.3 32.8 %all-gather.1 = bf16[1,4,512]{1,0,2:T(2,128)(2,1)S(1)} all-gather(bf16[1,4,64]{1,0,2:T(2,128)(2,1)S(1)} %copy.67), channel_id=3, replica_groups=mesh['dp'=2,'mp'=4,'width'=4] {'dp','width'}, dimensions={2}, use_global_device_ids=true | all-gather | bytes 4608 | tf_op jit(solution)/shard_map/all_gather | solution.py:289
  46.9 31.0 %all-gather = bf16[1,2,512]{1,0,2:T(2,128)(2,1)S(1)} all-gather(bf16[1,2,64]{1,0,2:T(2,128)(2,1)S(1)} %copy.66), channel_id=2, replica_groups=mesh['dp'=2,'mp'=4,'width'=4] {'dp','width'}, dimensions={2}, use_global_device_ids=true | all-gather | bytes 2304 | tf_op jit(solution)/shard_map/all_gather | solution.py:288
  82.3 32.2 %all-gather.2 = bf16[1,512,3,128]{3,1,2,0:T(8,128)(2,1)S(1)} all-gather(bf16[1,64,3,128]{3,1,2,0:T(8,128)(2,1)S(1)} %get-tuple-element.126), channel_id=4, replica_groups=mesh['dp'=2,'mp'=4,'width'=4] {'dp','width'}, dimensions={1}, use_global_device_ids=true | all-gather | bytes 442368 | tf_op jit(solution)/shard_map/all_gather | solution.py:290
  114.9 31.2 %all-gather.8 = bf16[1,4,512]{1,0,2:T(2,128)(2,1)S(1)} all-gather(bf16[1,4,64]{1,0,2:T(2,128)(2,1)S(1)} %copy.69), channel_id=10, replica_groups=mesh['dp'=2,'mp'=4,'width'=4] {'dp','width'}, dimensions={2}, use_global_device_ids=true | all-gather | bytes 4608 | tf_op jit(solution)/shard_map/all_gather | solution.py:289
  146.1 30.8 %all-gather.3 = bf16[1,128,512]{1,2,0:T(8,128)(2,1)S(1)} all-gather(bf16[1,128,64]{1,2,0:T(8,128)(2,1)S(1)} %get-tuple-element.130), channel_id=5, replica_groups=mesh['dp'=2,'mp'=4,'width'=4] {'dp','width'}, dimensions={2}, use_global_device_ids=true | all-gather | bytes 147456 | tf_op jit(solution)/shard_map/all_gather | solution.py:291
  177.6 31.2 %all-gather.4 = bf16[1,2,512,128]{3,2,1,0:T(8,128)(2,1)S(1)} all-gather(bf16[1,2,64,128]{3,2,1,0:T(8,128)(2,1)S(1)} %get-tuple-element.128), channel_id=6, replica_groups=mesh['dp'=2,'mp'=4,'width'=4] {'dp','width'}, dimensions={2}, use_global_device_ids=true | all-gather | bytes 294912 | tf_op jit(solution)/shard_map/all_gather | solution.py:292
  208.9 3.5 slice_reduce_fusion.2
  228.1 26.3 %reduce-scatter.39.cloned.1.call-done = bf16[256,512]{1,0:T(8,128)(2,1)} async-done(((bf16[1024,512]{1,0:T(8,128)(2,1)}), bf16[256,512]{1,0:T(8,128)(2,1)}) %reduce-scatter.39.cloned.1.call-update) | async-done | bytes 262160 | tf_op jit(solution)/shard_map/reduce_scatter | solution.py:32
  258.0 15.3 all-gather.39.cloned.1.call-done
  287.5 25.0 %reduce-scatter.47.cloned.1.call-done = bf16[256,512]{1,0:T(8,128)(2,1)} async-done(((bf16[1024,512]{1,0:T(8,128)(2,1)}), bf16[256,512]{1,0:T(8,128)(2,1)}) %reduce-scatter.47.cloned.1.call-update) | async-done | bytes 262160 | tf_op jit(solution)/shard_map/reduce_scatter | solution.py:32
  318.9 32.4 %all-gather.6 = bf16[1,512,512]{1,2,0:T(8,128)(2,1)S(1)} all-gather(bf16[1,512,64]{1,2,0:T(8,128)(2,1)S(1)} %get-tuple-element.124), channel_id=8, replica_groups=mesh['dp'=2,'mp'=4,'width'=4] {'dp','width'}, dimensions={2}, use_global_device_ids=true | all-gather | bytes 589824 | tf_op jit(solution)/shard_map/all_gather | solution.py:294
  351.4 32.1 %all-gather.5 = bf16[1,512,512]{2,1,0:T(8,128)(2,1)S(1)} all-gather(bf16[1,64,512]{2,1,0:T(8,128)(2,1)S(1)} %get-tuple-element.122), channel_id=7, replica_groups=mesh['dp'=2,'mp'=4,'width'=4] {'dp','width'}, dimensions={1}, use_global_device_ids=true | all-gather | bytes 589824 | tf_op jit(solution)/shard_map/all_gather | solution.py:293
  396.9 31.3 %all-gather.7 = bf16[1,2,512]{1,0,2:T(2,128)(2,1)S(1)} all-gather(bf16[1,2,64]{1,0,2:T(2,128)(2,1)S(1)} %copy.68), channel_id=9, replica_groups=mesh['dp'=2,'mp'=4,'width'=4] {'dp','width'}, dimensions={2}, use_global_device_ids=true | all-gather | bytes 2304 | tf_op jit(solution)/shard_map/all_gather | solution.py:288
  428.2 3.4 fusion.328
  434.4 9.3 reduce-scatter.49.cloned.1.call-done
  447.7 31.9 %all-gather.9 = bf16[1,512,3,128]{3,1,2,0:T(8,128)(2,1)S(1)} all-gather(bf16[1,64,3,128]{3,1,2,0:T(8,128)(2,1)S(1)} %get-tuple-element.125), channel_id=11, replica_groups=mesh['dp'=2,'mp'=4,'width'=4] {'dp','width'}, dimensions={1}, use_global_device_ids=true | all-gather | bytes 442368 | tf_op jit(solution)/shard_map/all_gather | solution.py:290
  479.9 30.9 %all-gather.10 = bf16[1,128,512]{1,2,0:T(8,128)(2,1)S(1)} all-gather(bf16[1,128,64]{1,2,0:T(8,128)(2,1)S(1)} %copy-done.161), channel_id=12, replica_groups=mesh['dp'=2,'mp'=4,'width'=4] {'dp','width'}, dimensions={2}, use_global_device_ids=true | all-gather | bytes 147456 | tf_op jit(solution)/shard_map/all_gather | solution.py:291
  510.7 33.3 %all-gather.11 = bf16[1,2,512,128]{3,2,1,0:T(8,128)(2,1)} all-gather(bf16[1,2,64,128]{3,2,1,0:T(8,128)(2,1)S(1)} %copy-done.156), channel_id=13, replica_groups=mesh['dp'=2,'mp'=4,'width'=4] {'dp','width'}, dimensions={2}, use_global_device_ids=true | all-gather | bytes 294912 | tf_op jit(solution)/shard_map/all_gather | solution.py:292
  544.0 4.1 slice_reduce_fusion
  550.1 3.7 fusion.417
  553.7 3.5 fusion.418
  562.3 3.6 fusion.420
  587.9 12.7 reduce-scatter.43.cloned.1.call-done
  602.5 26.2 %reduce-scatter.51.cloned.1.call-done = bf16[256,512]{1,0:T(8,128)(2,1)} async-done(((bf16[1024,512]{1,0:T(8,128)(2,1)}), bf16[256,512]{1,0:T(8,128)(2,1)}) %reduce-scatter.51.cloned.1.call-update) | async-done | bytes 262160 | tf_op jit(solution)/shard_map/reduce_scatter | solution.py:32
  635.5 34.8 %all-gather.13 = bf16[1,512,512]{1,2,0:T(8,128)(2,1)} all-gather(bf16[1,512,64]{1,2,0:T(8,128)(2,1)} %get-tuple-element.123), channel_id=15, replica_groups=mesh['dp'=2,'mp'=4,'width'=4] {'dp','width'}, dimensions={2}, use_global_device_ids=true | all-gather | bytes 589824 | tf_op jit(solution)/shard_map/all_gather | solution.py:294
  670.4 34.6 %all-gather.12 = bf16[1,512,512]{2,1,0:T(8,128)(2,1)} all-gather(bf16[1,64,512]{2,1,0:T(8,128)(2,1)} %get-tuple-element.121), channel_id=14, replica_groups=mesh['dp'=2,'mp'=4,'width'=4] {'dp','width'}, dimensions={1}, use_global_device_ids=true | all-gather | bytes 589824 | tf_op jit(solution)/shard_map/all_gather | solution.py:293
  710.5 3.5 convert_reduce_fusion.12
  723.8 21.0 reduce-scatter.55.cloned.1.call-done
  747.8 25.0 %reduce-scatter.45.cloned.1.call-done = bf16[256,512]{1,0:T(8,128)(2,1)} async-done(((bf16[1024,512]{1,0:T(8,128)(2,1)}), bf16[256,512]{1,0:T(8,128)(2,1)}) %reduce-scatter.45.cloned.1.call-update) | async-done | bytes 262160 | tf_op jit(solution)/shard_map/reduce_scatter | solution.py:32
  780.1 11.5 all-gather.45.cloned.1.call-done
  797.1 13.3 all-gather.49.cloned.1.call-done
  812.8 16.5 all-gather.55.cloned.1.call-done
  829.3 3.7 convert_reduce_fusion.10
  844.3 3.6 multiply_reduce_fusion.7
  858.6 3.3 fusion.56
  871.1 26.4 %reduce-scatter.53.cloned.1.call-done = bf16[256,512]{1,0:T(8,128)(2,1)} async-done(((bf16[1024,512]{1,0:T(8,128)(2,1)}), bf16[256,512]{1,0:T(8,128)(2,1)}) %reduce-scatter.53.cloned.1.call-update) | async-done | bytes 262160 | tf_op jit(solution)/shard_map/reduce_scatter | solution.py:32
  899.7 25.3 %reduce-scatter.57.cloned.1.call-done = bf16[256,512]{1,0:T(8,128)(2,1)} async-done(((bf16[1024,512]{1,0:T(8,128)(2,1)}), bf16[256,512]{1,0:T(8,128)(2,1)}) %reduce-scatter.57.cloned.1.call-update) | async-done | bytes 262160 | tf_op jit(solution)/shard_map/reduce_scatter | solution.py:42
  931.4 16.8 all-gather.57.cloned.1.call-done
  950.0 3.5 multiply_reduce_fusion.3
  967.4 24.2 %reduce-scatter.65.cloned.1.call-done = bf16[256,512]{1,0:T(8,128)(2,1)} async-done(((bf16[1024,512]{1,0:T(8,128)(2,1)}), bf16[256,512]{1,0:T(8,128)(2,1)}) %reduce-scatter.65.cloned.1.call-update) | async-done | bytes 262160 | tf_op jit(solution)/shard_map/reduce_scatter | solution.py:42
  997.1 13.4 all-gather.51.cloned.1.call-done
  1018.5 10.3 all-gather.59.cloned.1.call-done
  1036.0 20.6 reduce-scatter.59.cloned.1.call-done
  1056.6 28.2 %reduce-scatter.67.cloned.1.call-done = bf16[256,512]{1,0:T(8,128)(2,1)} async-done(((bf16[1024,512]{1,0:T(8,128)(2,1)}), bf16[256,512]{1,0:T(8,128)(2,1)}) %reduce-scatter.67.cloned.1.call-update) | async-done | bytes 262160 | tf_op jit(solution)/shard_map/reduce_scatter | solution.py:42
  1092.5 3.3 fusion.424
  1097.8 3.7 convolution_add_fusion.10
  1148.5 3.5 multiply_reduce_fusion.1
  1184.1 6.4 reduce-scatter.93.cloned.1.call-done
  1191.4 62.8 %reduce-scatter.97.cloned.1.call-done = f32[64,4]{1,0:T(8,128)} async-done(((f32[512,4]{1,0:T(8,128)}), f32[64,4]{1,0:T(8,128)}) %reduce-scatter.97.cloned.1.call-update) | async-done | bytes 1040
  1255.1 65.0 %reduce-scatter.85.cloned.1.call-done = f32[64,512]{1,0:T(8,128)} async-done(((f32[512,512]{1,0:T(8,128)}), f32[64,512]{1,0:T(8,128)}) %reduce-scatter.85.cloned.1.call-update) | async-done | bytes 131088 | tf_op jit(solution)/shard_map/reduce_scatter | solution.py:336
  1320.1 66.3 %reduce-scatter.83.cloned.1.call-done = f32[64,512]{1,0:T(8,128)} async-done(((f32[512,512]{1,0:T(8,128)}), f32[64,512]{1,0:T(8,128)}) %reduce-scatter.83.cloned.1.call-update) | async-done | bytes 131088 | tf_op jit(solution)/shard_map/reduce_scatter | solution.py:336
  1388.0 64.2 %reduce-scatter.89.cloned.1.call-done = f32[512,64]{0,1:T(8,128)} async-done(((f32[512,512]{0,1:T(8,128)}), f32[512,64]{0,1:T(8,128)}) %reduce-scatter.89.cloned.1.call-update) | async-done | bytes 131088 | tf_op jit(solution)/shard_map/reduce_scatter | solution.py:339
  1452.3 66.2 %reduce-scatter.87.cloned.1.call-done = f32[512,64]{0,1:T(8,128)} async-done(((f32[512,512]{0,1:T(8,128)}), f32[512,64]{0,1:T(8,128)}) %reduce-scatter.87.cloned.1.call-update) | async-done | bytes 131088 | tf_op jit(solution)/shard_map/reduce_scatter | solution.py:339
  1520.2 61.7 %reduce-scatter.77.cloned.1.call-done = f32[128,64]{0,1:T(8,128)} async-done(((f32[128,512]{0,1:T(8,128)}), f32[128,64]{0,1:T(8,128)}) %reduce-scatter.77.cloned.1.call-update) | async-done | bytes 32784 | tf_op jit(solution)/shard_map/reduce_scatter | solution.py:330
  1581.9 63.6 %reduce-scatter.75.cloned.1.call-done = f32[128,64]{0,1:T(8,128)} async-done(((f32[128,512]{0,1:T(8,128)}), f32[128,64]{0,1:T(8,128)}) %reduce-scatter.75.cloned.1.call-update) | async-done | bytes 32784 | tf_op jit(solution)/shard_map/reduce_scatter | solution.py:330
  1646.9 62.8 %reduce-scatter.81.cloned.1.call-done = f32[2,64,128]{2,1,0:T(8,128)} async-done(((f32[2,512,128]{2,1,0:T(8,128)}), f32[2,64,128]{2,1,0:T(8,128)}) %reduce-scatter.81.cloned.1.call-update) | async-done | bytes 65552 | tf_op jit(solution)/shard_map/reduce_scatter | solution.py:333
  1709.6 64.7 %reduce-scatter.79.cloned.1.call-done = f32[2,64,128]{2,1,0:T(8,128)} async-done(((f32[2,512,128]{2,1,0:T(8,128)}), f32[2,64,128]{2,1,0:T(8,128)}) %reduce-scatter.79.cloned.1.call-update) | async-done | bytes 65552 | tf_op jit(solution)/shard_map/reduce_scatter | solution.py:333
  1775.8 64.0 %reduce-scatter.73.cloned.1.call-done = f32[64,3,128]{2,0,1:T(8,128)} async-done(((f32[512,3,128]{2,0,1:T(8,128)}), f32[64,3,128]{2,0,1:T(8,128)}) %reduce-scatter.73.cloned.1.call-update) | async-done | bytes 98320 | tf_op jit(solution)/shard_map/reduce_scatter | solution.py:327
  1839.9 66.0 %reduce-scatter.71.cloned.1.call-done = f32[64,3,128]{2,0,1:T(8,128)} async-done(((f32[512,3,128]{2,0,1:T(8,128)}), f32[64,3,128]{2,0,1:T(8,128)}) %reduce-scatter.71.cloned.1.call-update) | async-done | bytes 98320 | tf_op jit(solution)/shard_map/reduce_scatter | solution.py:327
  1907.5 24.7 %reduce-scatter.69.cloned.1.call-done = bf16[256,512]{1,0:T(8,128)(2,1)} async-done(((bf16[1024,512]{1,0:T(8,128)(2,1)}), bf16[256,512]{1,0:T(8,128)(2,1)}) %reduce-scatter.69.cloned.1.call-update) | async-done | bytes 262160 | tf_op jit(solution)/shard_map/reduce_scatter | solution.py:42
  1932.1 28.1 %reduce-scatter.61.cloned.1.call-done = bf16[256,512]{1,0:T(8,128)(2,1)} async-done(((bf16[1024,512]{1,0:T(8,128)(2,1)}), bf16[256,512]{1,0:T(8,128)(2,1)}) %reduce-scatter.61.cloned.1.call-update) | async-done | bytes 262160 | tf_op jit(solution)/shard_map/reduce_scatter | solution.py:42
  1967.0 58.8 %reduce-scatter.91.cloned.1.call-done = f32[64,2]{1,0:T(8,128)} async-done(((f32[512,2]{1,0:T(8,128)}), f32[64,2]{1,0:T(8,128)}) %reduce-scatter.91.cloned.1.call-update) | async-done | bytes 528
  2026.7 62.7 %reduce-scatter.95.cloned.1.call-done = f32[64,4]{1,0:T(8,128)} async-done(((f32[512,4]{1,0:T(8,128)}), f32[64,4]{1,0:T(8,128)}) %reduce-scatter.95.cloned.1.call-update) | async-done | bytes 1040
  2090.2 6.3 all-reduce
  (943 shorter events, 324.2 us)
Async XLA Ops:
  7.2 206.5 %all-gather.31.cloned.1.call-start = ((), (), s32[]{:S(2)}) async-start(), calls=%async_computation.30 | async-start | bytes 1310720 | tf_op jit(solution)/shard_map/all_gather | solution.py:28
  80.7 174.9 %copy-start.158 = (f32[512]{0:T(512)}, f32[512]{0:T(512)S(1)}, u32[]{:S(2)}) copy-start(f32[512]{0:T(512)S(1)} %get-tuple-element.53) | copy-start | bytes 6148
  80.7 234.7 %copy-start.175 = (f32[512]{0:T(512)}, f32[512]{0:T(512)S(1)}, u32[]{:S(2)}) copy-start(f32[512]{0:T(512)S(1)} %get-tuple-element.52) | copy-start | bytes 6148
  81.7 172.7 %reduce-scatter.39.cloned.1.call-start = ((), (), s32[]{:S(2)}) async-start(), calls=%async_computation.31 | async-start | bytes 1310720 | tf_op jit(solution)/shard_map/reduce_scatter | solution.py:32
  208.8 184.4 %copy-start.60 = (bf16[1,2,512,128]{3,2,1,0:T(8,128)(2,1)}, bf16[1,2,512,128]{3,2,1,0:T(8,128)(2,1)S(1)}, u32[]{:S(2)}) copy-start(bf16[1,2,512,128]{3,2,1,0:T(8,128)(2,1)S(1)} %all-gather.4) | copy-start | bytes 786436
  228.1 45.3 %all-gather.39.cloned.1.call-start = ((), (), s32[]{:S(2)}) async-start(), calls=%async_computation.38 | async-start | bytes 1310720 | tf_op jit(solution)/shard_map/all_gather | solution.py:28
  256.5 56.0 %reduce-scatter.47.cloned.1.call-start = ((), (), s32[]{:S(2)}) async-start(), calls=%async_computation.39 | async-start | bytes 1310720 | tf_op jit(solution)/shard_map/reduce_scatter | solution.py:32
  287.4 96.0 %all-gather.33.cloned.1.call-start = ((), (), s32[]{:S(2)}) async-start(), calls=%async_computation.32 | async-start | bytes 1310720 | tf_op jit(solution)/shard_map/all_gather | solution.py:28
  317.5 72.8 %all-gather.41.cloned.1.call-start = ((), (), s32[]{:S(2)}) async-start(), calls=%async_computation.40 | async-start | bytes 1310720 | tf_op jit(solution)/shard_map/all_gather | solution.py:28
  318.2 116.1 %reduce-scatter.41.cloned.1.call-start = ((), (), s32[]{:S(2)}) async-start(), calls=%async_computation.33 | async-start | bytes 1310720 | tf_op jit(solution)/shard_map/reduce_scatter | solution.py:32
  389.8 53.8 %reduce-scatter.49.cloned.1.call-start = ((), (), s32[]{:S(2)}) async-start(), calls=%async_computation.41 | async-start | bytes 1310720 | tf_op jit(solution)/shard_map/reduce_scatter | solution.py:32
  396.8 151.4 %all-gather.35.cloned.1.call-start = ((), (), s32[]{:S(2)}) async-start(), calls=%async_computation.34 | async-start | bytes 1310720 | tf_op jit(solution)/shard_map/all_gather | solution.py:28
  447.0 110.2 %all-gather.43.cloned.1.call-start = ((), (), s32[]{:S(2)}) async-start(), calls=%async_computation.42 | async-start | bytes 1310720 | tf_op jit(solution)/shard_map/all_gather | solution.py:28
  447.6 153.0 %reduce-scatter.43.cloned.1.call-start = ((), (), s32[]{:S(2)}) async-start(), calls=%async_computation.35 | async-start | bytes 1310720 | tf_op jit(solution)/shard_map/reduce_scatter | solution.py:32
  575.8 52.9 %reduce-scatter.51.cloned.1.call-start = ((), (), s32[]{:S(2)}) async-start(), calls=%async_computation.43 | async-start | bytes 1310720 | tf_op jit(solution)/shard_map/reduce_scatter | solution.py:32
  587.9 117.0 %all-gather.37.cloned.1.call-start = ((), (), s32[]{:S(2)}) async-start(), calls=%async_computation.36 | async-start | bytes 1310720 | tf_op jit(solution)/shard_map/all_gather | solution.py:28
  632.4 78.2 %all-gather.47.cloned.1.call-start = ((), (), s32[]{:S(2)}) async-start(), calls=%async_computation.46 | async-start | bytes 1310720 | tf_op jit(solution)/shard_map/all_gather | solution.py:38
  635.5 109.3 %reduce-scatter.55.cloned.1.call-start = ((), (), s32[]{:S(2)}) async-start(), calls=%async_computation.47 | async-start | bytes 1310720 | tf_op jit(solution)/shard_map/reduce_scatter | solution.py:42
  719.9 53.0 %reduce-scatter.45.cloned.1.call-start = ((), (), s32[]{:S(2)}) async-start(), calls=%async_computation.37 | async-start | bytes 1310720 | tf_op jit(solution)/shard_map/reduce_scatter | solution.py:32
  722.6 69.0 %all-gather.45.cloned.1.call-start = ((), (), s32[]{:S(2)}) async-start(), calls=%async_computation.44 | async-start | bytes 1310720 | tf_op jit(solution)/shard_map/all_gather | solution.py:28
  723.2 87.1 %all-gather.49.cloned.1.call-start = ((), (), s32[]{:S(2)}) async-start(), calls=%async_computation.48 | async-start | bytes 1310720 | tf_op jit(solution)/shard_map/all_gather | solution.py:38
  777.5 51.8 %all-gather.55.cloned.1.call-start = ((), (), s32[]{:S(2)}) async-start(), calls=%async_computation.54 | async-start | bytes 1310720 | tf_op jit(solution)/shard_map/all_gather | solution.py:38
  778.2 91.1 %reduce-scatter.63.cloned.1.call-start = ((), (), s32[]{:S(2)}) async-start(), calls=%async_computation.55 | async-start | bytes 1310720 | tf_op jit(solution)/shard_map/reduce_scatter | solution.py:42
  844.2 53.3 %reduce-scatter.53.cloned.1.call-start = ((), (), s32[]{:S(2)}) async-start(), calls=%async_computation.45 | async-start | bytes 1310720 | tf_op jit(solution)/shard_map/reduce_scatter | solution.py:32
  856.1 68.9 %reduce-scatter.57.cloned.1.call-start = ((), (), s32[]{:S(2)}) async-start(), calls=%async_computation.49 | async-start | bytes 1310720 | tf_op jit(solution)/shard_map/reduce_scatter | solution.py:42
  868.1 80.1 %all-gather.57.cloned.1.call-start = ((), (), s32[]{:S(2)}) async-start(), calls=%async_computation.56 | async-start | bytes 1310720 | tf_op jit(solution)/shard_map/all_gather | solution.py:38
  931.3 60.3 %reduce-scatter.65.cloned.1.call-start = ((), (), s32[]{:S(2)}) async-start(), calls=%async_computation.57 | async-start | bytes 1310720 | tf_op jit(solution)/shard_map/reduce_scatter | solution.py:42
  966.6 43.9 %all-gather.51.cloned.1.call-start = ((), (), s32[]{:S(2)}) async-start(), calls=%async_computation.50 | async-start | bytes 1310720 | tf_op jit(solution)/shard_map/all_gather | solution.py:38
  967.4 61.4 %all-gather.59.cloned.1.call-start = ((), (), s32[]{:S(2)}) async-start(), calls=%async_computation.58 | async-start | bytes 1310720 | tf_op jit(solution)/shard_map/all_gather | solution.py:38
  996.7 59.9 %reduce-scatter.59.cloned.1.call-start = ((), (), s32[]{:S(2)}) async-start(), calls=%async_computation.51 | async-start | bytes 1310720 | tf_op jit(solution)/shard_map/reduce_scatter | solution.py:42
  1018.4 66.4 %reduce-scatter.67.cloned.1.call-start = ((), (), s32[]{:S(2)}) async-start(), calls=%async_computation.59 | async-start | bytes 1310720 | tf_op jit(solution)/shard_map/reduce_scatter | solution.py:42
  1035.9 85.6 %all-gather.53.cloned.1.call-start = ((), (), s32[]{:S(2)}) async-start(), calls=%async_computation.52 | async-start | bytes 1310720 | tf_op jit(solution)/shard_map/all_gather | solution.py:38
  1090.3 35.6 %all-gather.61.cloned.1.call-start = ((), (), s32[]{:S(2)}) async-start(), calls=%async_computation.60 | async-start | bytes 1310720 | tf_op jit(solution)/shard_map/all_gather | solution.py:38
  1092.3 98.3 %reduce-scatter.93.cloned.1.call-start = ((), (), s32[]{:S(2)}) async-start(), calls=%async_computation.73 | async-start | bytes 294912
  1096.8 157.5 %reduce-scatter.97.cloned.1.call-start = ((), (), s32[]{:S(2)}) async-start(), calls=%async_computation.75 | async-start | bytes 294912
  1097.8 222.3 %reduce-scatter.85.cloned.1.call-start = ((), (), s32[]{:S(2)}) async-start(), calls=%async_computation.69 | async-start | bytes 1179648 | tf_op jit(solution)/shard_map/reduce_scatter | solution.py:336
  1101.5 284.8 %reduce-scatter.83.cloned.1.call-start = ((), (), s32[]{:S(2)}) async-start(), calls=%async_computation.68 | async-start | bytes 1179648 | tf_op jit(solution)/shard_map/reduce_scatter | solution.py:336
  1105.5 346.8 %reduce-scatter.89.cloned.1.call-start = ((), (), s32[]{:S(2)}) async-start(), calls=%async_computation.71 | async-start | bytes 1179648 | tf_op jit(solution)/shard_map/reduce_scatter | solution.py:339
  1110.6 407.8 %reduce-scatter.87.cloned.1.call-start = ((), (), s32[]{:S(2)}) async-start(), calls=%async_computation.70 | async-start | bytes 1179648 | tf_op jit(solution)/shard_map/reduce_scatter | solution.py:339
  1115.7 466.3 %reduce-scatter.77.cloned.1.call-start = ((), (), s32[]{:S(2)}) async-start(), calls=%async_computation.65 | async-start | bytes 294912 | tf_op jit(solution)/shard_map/reduce_scatter | solution.py:330
  1121.5 524.0 %reduce-scatter.75.cloned.1.call-start = ((), (), s32[]{:S(2)}) async-start(), calls=%async_computation.64 | async-start | bytes 294912 | tf_op jit(solution)/shard_map/reduce_scatter | solution.py:330
  1128.5 581.1 %reduce-scatter.81.cloned.1.call-start = ((), (), s32[]{:S(2)}) async-start(), calls=%async_computation.67 | async-start | bytes 589824 | tf_op jit(solution)/shard_map/reduce_scatter | solution.py:333
  1133.4 640.9 %reduce-scatter.79.cloned.1.call-start = ((), (), s32[]{:S(2)}) async-start(), calls=%async_computation.66 | async-start | bytes 589824 | tf_op jit(solution)/shard_map/reduce_scatter | solution.py:333
  1142.7 697.2 %reduce-scatter.73.cloned.1.call-start = ((), (), s32[]{:S(2)}) async-start(), calls=%async_computation.63 | async-start | bytes 884736 | tf_op jit(solution)/shard_map/reduce_scatter | solution.py:327
  1146.6 759.2 %reduce-scatter.71.cloned.1.call-start = ((), (), s32[]{:S(2)}) async-start(), calls=%async_computation.62 | async-start | bytes 884736 | tf_op jit(solution)/shard_map/reduce_scatter | solution.py:327
  1174.6 757.5 %reduce-scatter.69.cloned.1.call-start = ((), (), s32[]{:S(2)}) async-start(), calls=%async_computation.61 | async-start | bytes 1310720 | tf_op jit(solution)/shard_map/reduce_scatter | solution.py:42
  1179.5 780.8 %reduce-scatter.61.cloned.1.call-start = ((), (), s32[]{:S(2)}) async-start(), calls=%async_computation.53 | async-start | bytes 1310720 | tf_op jit(solution)/shard_map/reduce_scatter | solution.py:42
  1182.6 337.5 %copy-start.259 = (f32[128]{0:T(128)S(1)}, f32[128]{0:T(128)}, u32[]{:S(2)}) copy-start(f32[128]{0:T(128)} %get-tuple-element.66) | copy-start | bytes 1540
  1182.6 337.6 %copy-start.258 = (f32[128]{0:T(128)S(1)}, f32[128]{0:T(128)}, u32[]{:S(2)}) copy-start(f32[128]{0:T(128)} %get-tuple-element.62) | copy-start | bytes 1540
  1182.6 777.7 %copy-start.159 = (f32[512]{0:T(512)S(1)}, f32[512]{0:T(512)}, u32[]{:S(2)}) copy-start(f32[512]{0:T(512)} %copy-done.158) | copy-start | bytes 6148
  1182.6 777.6 %copy-start.170 = (f32[256]{0:T(256)S(1)}, f32[256]{0:T(256)}, u32[]{:S(2)}) copy-start(f32[256]{0:T(256)} %copy-done.169) | copy-start | bytes 3076
  1182.7 777.6 %copy-start.172 = (f32[256]{0:T(256)S(1)}, f32[256]{0:T(256)}, u32[]{:S(2)}) copy-start(f32[256]{0:T(256)} %copy-done.171) | copy-start | bytes 3076
  1182.7 843.2 %reduce-scatter.91.cloned.1.call-start = ((), (), s32[]{:S(2)}) async-start(), calls=%async_computation.72 | async-start | bytes 294912
  1183.1 778.7 %copy-start.232 = (f32[256]{0:T(256)S(1)}, f32[256]{0:T(256)}, u32[]{:S(2)}) copy-start(f32[256]{0:T(256)} %copy-done.231) | copy-start | bytes 3076
  1183.1 778.7 %copy-start.234 = (f32[256]{0:T(256)S(1)}, f32[256]{0:T(256)}, u32[]{:S(2)}) copy-start(f32[256]{0:T(256)} %copy-done.233) | copy-start | bytes 3076
  1183.1 778.7 %copy-start.195 = (f32[256]{0:T(256)S(1)}, f32[256]{0:T(256)}, u32[]{:S(2)}) copy-start(f32[256]{0:T(256)} %copy-done.194) | copy-start | bytes 3076
  1183.1 778.7 %copy-start.197 = (f32[256]{0:T(256)S(1)}, f32[256]{0:T(256)}, u32[]{:S(2)}) copy-start(f32[256]{0:T(256)} %copy-done.196) | copy-start | bytes 3076
  1184.1 779.4 %copy-start.250 = (f32[512]{0:T(512)S(1)}, f32[512]{0:T(512)}, u32[]{:S(2)}) copy-start(f32[512]{0:T(512)} %get-tuple-element.12) | copy-start | bytes 6148
  1184.1 779.4 %copy-start.251 = (f32[512]{0:T(512)S(1)}, f32[512]{0:T(512)}, u32[]{:S(2)}) copy-start(f32[512]{0:T(512)} %get-tuple-element.29) | copy-start | bytes 6148
  1388.0 576.5 %copy-start.45 = (f32[256,512]{1,0:T(8,128)S(1)}, f32[256,512]{1,0:T(8,128)}, u32[]{:S(2)}) copy-start(f32[256,512]{1,0:T(8,128)} %copy-done.44) | copy-start | bytes 1572868
  1388.0 576.5 %copy-start.47 = (f32[256,512]{1,0:T(8,128)S(1)}, f32[256,512]{1,0:T(8,128)}, u32[]{:S(2)}) copy-start(f32[256,512]{1,0:T(8,128)} %get-tuple-element.87) | copy-start | bytes 1572868
  1388.0 576.5 %copy-start.49 = (f32[256,512]{1,0:T(8,128)S(1)}, f32[256,512]{1,0:T(8,128)}, u32[]{:S(2)}) copy-start(f32[256,512]{1,0:T(8,128)} %copy-done.48) | copy-start | bytes 1572868
  1388.0 576.5 %copy-start.50 = (f32[256,512]{1,0:T(8,128)S(1)}, f32[256,512]{1,0:T(8,128)}, u32[]{:S(2)}) copy-start(f32[256,512]{1,0:T(8,128)} %get-tuple-element.105) | copy-start | bytes 1572868
  1964.5 124.9 %reduce-scatter.95.cloned.1.call-start = ((), (), s32[]{:S(2)}) async-start(), calls=%async_computation.74 | async-start | bytes 294912
  (246 other events, 3616.1 us)
Sparse Core Ops, SparseCore 0:
  81.8 18.4 all-gather.30
  228.2 26.1 reduce-scatter.38
  256.6 16.6 all-gather.38
  287.5 24.8 reduce-scatter.46
  317.6 16.7 all-gather.32
  336.4 16.7 all-gather.40
  389.9 25.4 reduce-scatter.40
  418.7 24.8 reduce-scatter.48
  447.2 16.7 all-gather.34
  465.9 16.7 all-gather.42
  576.0 24.6 reduce-scatter.42
  603.8 24.8 reduce-scatter.50
  632.5 16.7 all-gather.36
  651.2 16.7 all-gather.46
  720.0 24.7 reduce-scatter.54
  747.9 24.8 reduce-scatter.44
  774.9 16.7 all-gather.44
  793.6 16.7 all-gather.48
  812.5 16.7 all-gather.54
  844.4 24.8 reduce-scatter.62
  872.6 24.8 reduce-scatter.52
  900.0 24.9 reduce-scatter.56
  931.4 16.7 all-gather.56
  966.8 24.8 reduce-scatter.64
  993.8 16.7 all-gather.50
  1012.0 16.7 all-gather.58
  1031.7 24.8 reduce-scatter.58
  1059.9 24.8 reduce-scatter.66
  1090.4 16.7 all-gather.52
  1109.2 16.7 all-gather.60
  1129.3 61.2 reduce-scatter.92
  1193.9 60.2 reduce-scatter.96
  1257.5 62.5 reduce-scatter.84
  1323.8 62.4 reduce-scatter.82
  1389.7 62.4 reduce-scatter.88
  1455.9 62.5 reduce-scatter.86
  1521.6 60.2 reduce-scatter.76
  1585.2 60.1 reduce-scatter.74
  1648.7 60.9 reduce-scatter.80
  1713.3 60.9 reduce-scatter.78
  1777.6 62.1 reduce-scatter.72
  1843.6 62.2 reduce-scatter.70
  1908.2 23.8 reduce-scatter.68
  1935.4 24.8 reduce-scatter.60
  1964.6 61.2 reduce-scatter.90
  2029.0 60.2 reduce-scatter.94
where the time goes:
time: 2110 us; the launch traced here: 2100 us
  waiting for transfers between devices  1260 us (60%)
  blocking collectives  457 us (22%)
  matrix products  176 us (8%)
  other arithmetic  133 us (6%)
  local copies, waits for them, and re-layouts  54 us (3%)
    unnamed x50, waiting for transfers between devices  194 us
    reduce_scatter x8, waiting for transfers between devices, collect_grads(): lax.psum_scatter(branch_term.astype(jnp.bfloat16), 'mp', scatter_dimensio...  173 us
    reduce_scatter x8, waiting for transfers between devices, collect_rows(): lax.psum_scatter(branch_term.astype(jnp.bfloat16), 'mp', scatter_dimensio...  151 us
    reduce_scatter x2, waiting for transfers between devices, on_device(): lax.psum_scatter(grad_terms[5], ('dp', 'width'), scatter_dimension=0, til...  131 us
    reduce_scatter x2, waiting for transfers between devices, on_device(): lax.psum_scatter(grad_terms[6], ('dp', 'width'), scatter_dimension=1, til...  130 us
    reduce_scatter x2, waiting for transfers between devices, on_device(): lax.psum_scatter(grad_terms[2], ('dp', 'width'), scatter_dimension=0, til...  130 us
    reduce_scatter x2, waiting for transfers between devices, on_device(): lax.psum_scatter(grad_terms[4], ('dp', 'width'), scatter_dimension=1, til...  127 us
    reduce_scatter x2, waiting for transfers between devices, on_device(): lax.psum_scatter(grad_terms[3], ('dp', 'width'), scatter_dimension=1, til...  125 us
  transfers between devices with their start and end apart: 46, of which 37 were waited for; matrix products, arithmetic and copies ran while one was open for 10% of the time, Pallas kernels for 0%

commit v1 on v0

v1 whole, which is shorter than its diff:
```python
import functools

import jax
import jax.numpy as jnp
from jax import lax
from jax.experimental import pallas as pl
from jax.experimental.pallas import tpu as pltpu
from jax.sharding import PartitionSpec as P

HEAD_DIM = 64
LANE = 128
NORM_EPS = 1e-05
SPAN = 256

F32 = jnp.float32
BF16 = jnp.bfloat16


def nn(a, b):
    return jnp.dot(a, b, preferred_element_type=F32)


def nt(a, b):
    return lax.dot_general(a, b, (((1,), (1,)), ((), ())), preferred_element_type=F32)


def tn(a, b):
    return lax.dot_general(a, b, (((0,), (0,)), ((), ())), preferred_element_type=F32)


def sds(shape, dtype):
    return jax.ShapeDtypeStruct(shape, dtype)


def call(body, name, out_shape, args, smem=0, scratch=(), flops=0):
    specs = [pl.BlockSpec(memory_space=pltpu.SMEM)] * smem
    specs += [pl.BlockSpec(memory_space=pltpu.VMEM)] * (len(args) - smem)
    nbytes = sum(a.size * a.dtype.itemsize for a in args)
    nbytes += sum(o.size * o.dtype.itemsize for o in jax.tree.leaves(out_shape))
    return pl.pallas_call(
        body,
        name=name,
        out_shape=out_shape,
        in_specs=specs,
        out_specs=jax.tree.map(lambda _: pl.BlockSpec(memory_space=pltpu.VMEM), out_shape),
        scratch_shapes=list(scratch),
        cost_estimate=pl.CostEstimate(flops=flops, bytes_accessed=nbytes, transcendentals=0),
        compiler_params=pltpu.CompilerParams(vmem_limit_bytes=56 * 2**20),
    )(*args)


def col(start):
    return pl.multiple_of(start, LANE)


def unpack_body(order, plan, per, me_ref, *refs):
    parts, outs = refs[: len(order)], refs[len(order) :]
    me_m, me_d = me_ref[0], me_ref[1]
    for ref, slots in zip(parts, order):
        for at, (mx, dx) in enumerate(slots):
            m = jnp.bitwise_xor(me_m, mx)
            rows = pl.ds(pl.multiple_of(jnp.bitwise_xor(me_d, dx) * per, per), per)
            for b, (which, stride, offset) in enumerate(plan):
                block = ref[at, b * per : (b + 1) * per, :]
                if stride is None:
                    if mx == 0:
                        outs[which][rows, :] = block
                else:
                    outs[which][rows, pl.ds(col(m * stride + offset), LANE)] = block


PLAN_Q = [(0, 512, 0), (0, 512, 128), (0, 512, 256), (0, 512, 384), (1, None, 0)]
PLAN_U = [(0, 128, 0), (1, 512, 0), (1, 512, 128), (1, 512, 256), (1, 512, 384)]
PLAN_D = PLAN_U


def unpack(parts, order, plan, per, me, model, mp_size):
    widths = {}
    for which, stride, _ in plan:
        widths[which] = LANE if stride is None else stride * mp_size
    shapes = [sds((model, widths[w]), BF16) for w in sorted(widths)]
    return call(
        functools.partial(unpack_body, order, plan, per),
        "unpack",
        shapes,
        [me] + parts,
        smem=1,
    )


def norm_parts(x):
    mean = jnp.mean(x, axis=1, keepdims=True)
    centred = x - mean
    rstd = lax.rsqrt(jnp.mean(centred * centred, axis=1, keepdims=True) + NORM_EPS)
    return centred * rstd, rstd


def sigmoid(v):
    return 1.0 / (1.0 + jnp.exp(-v))


def first_body(mp_size, me_ref, x_ref, par_ref, wq_ref, n_ref, s1_ref, par_t_ref, *a_refs):
    me_m = me_ref[0]
    par_t = par_ref[...].astype(F32).T[:8]
    par_t_ref[...] = par_t
    xhat, _ = norm_parts(x_ref[...].astype(F32))
    n = (xhat * par_t[0:1] + par_t[2:3]).astype(BF16)
    n_ref[...] = n
    for mx in range(mp_size):
        m = jnp.bitwise_xor(me_m, mx)
        y = nn(n_ref[...], wq_ref[:, pl.ds(col(m * 512), 512)])
        a_refs[mx][...] = y[:, :384].astype(BF16)
        cols = pl.ds(col(m * LANE), LANE)
        s1_ref[:, cols] = sigmoid(y[:, 384:] + par_t_ref[3:4, cols])


def first(me, x, par, wq, mp_size):
    rows, model = x.shape
    out = [sds((rows, model), BF16), sds((rows, model), F32), sds((8, model), F32)]
    out += [sds((rows, 384), BF16)] * mp_size
    return call(
        functools.partial(first_body, mp_size),
        "first",
        out,
        [me, x, par, wq],
        smem=1,
        flops=2 * rows * wq.size,
    )


def seg_bounds(seg_ref, row, q_at, q_spans):
    first_id = seg_ref[row, q_at * SPAN]
    first_id = jnp.where(first_id < 0, 1 << 20, first_id)
    low = jnp.int32(0)
    for kb in range(q_spans - 1):
        last_id = seg_ref[row, (kb + 1) * SPAN - 1]
        last_id = jnp.where(last_id < 0, 1 << 20, last_id)
        low += jnp.where((kb < q_at) & (last_id < first_id), 1, 0)
    return low


def allowed_t(segc_ref, segr_ref, row, k0, q0, spans):
    keys = spans * SPAN
    seg_k = segc_ref[row, pl.ds(k0, keys), :]
    seg_q = segr_ref[row, :, pl.ds(q0, SPAN)]
    same = jnp.concatenate([seg_k == seg_q[:, :LANE], seg_k == seg_q[:, LANE:]], axis=1)
    tri = lax.broadcasted_iota(jnp.int32, (keys, SPAN), 0) - (keys - SPAN) <= (
        lax.broadcasted_iota(jnp.int32, (keys, SPAN), 1)
    )
    return same & tri


def attend_body(mp_size, me_ref, seg_ref, segc_ref, segr_ref, *refs):
    a_refs = refs[:mp_size]
    qkv_ref, lse_ref = refs[mp_size : mp_size + 2]
    o_refs = refs[mp_size + 2 : 2 * mp_size + 2]
    o_scr = refs[-1]
    rows = qkv_ref.shape[0]
    part = a_refs[0].shape[0] // rows
    me_m = me_ref[0]
    for mx in range(mp_size):
        at = pl.multiple_of(jnp.bitwise_xor(me_m, mx) * part, part)
        for r in range(rows):
            qkv_ref[r, pl.ds(at, part), :] = a_refs[mx][r * part : (r + 1) * part, :]
    q_spans = qkv_ref.shape[1] // SPAN

    def step(i, carry):
        r, q_at = i // q_spans, i % q_spans
        low = seg_bounds(seg_ref, r, q_at, q_spans)
        q0 = pl.multiple_of(q_at * SPAN, SPAN)
        k0 = pl.multiple_of(low * SPAN, SPAN)
        for spans in range(1, q_spans + 1):

            @pl.when(q_at - low + 1 == spans)
            def _():
                keys = spans * SPAN
                mask = allowed_t(segc_ref, segr_ref, r, k0, q0, spans)
                outs = []
                for h in range(2):
                    lo = h * HEAD_DIM
                    q = qkv_ref[r, pl.ds(q0, SPAN), lo : lo + HEAD_DIM] * jnp.asarray(
                        HEAD_DIM**-0.5, BF16
                    )
                    k = qkv_ref[r, pl.ds(k0, keys), 128 + lo : 128 + lo + HEAD_DIM]
                    v = qkv_ref[r, pl.ds(k0, keys), 256 + lo : 256 + lo + HEAD_DIM]
                    s = jnp.where(mask, nt(k, q), -1e30)
                    top = jnp.max(s, axis=0, keepdims=True)
                    p = jnp.exp(s - top)
                    total = jnp.sum(p, axis=0, keepdims=True)
                    lse_ref[r * 2 + h, :, pl.ds(q0, SPAN)] = top + jnp.log(total)
                    outs.append(tn(v, p.astype(BF16)) / total)
                o_scr[pl.ds(pl.multiple_of(i * SPAN, SPAN), SPAN), :] = (
                    jnp.concatenate(outs, axis=0).T.astype(BF16)
                )

        return carry

    lax.fori_loop(0, rows * q_spans, step, 0)
    length = qkv_ref.shape[1]
    for mx in range(mp_size):
        for r in range(rows):
            at = pl.multiple_of(r * length + jnp.bitwise_xor(me_m, mx) * part, part)
            o_refs[mx][r * part : (r + 1) * part, :] = o_scr[pl.ds(at, part), :]


def attend(me, seg, segc, segr, a_parts):
    mp_size = len(a_parts)
    rows, length = seg.shape
    local = a_parts[0].shape[0]
    out = [sds((rows, length, 384), BF16), sds((rows * 2, 1, length), F32)]
    out += [sds((local, LANE), BF16)] * mp_size
    return call(
        functools.partial(attend_body, mp_size),
        "attend",
        out,
        [me, seg, segc, segr] + a_parts,
        smem=2,
        scratch=[pltpu.VMEM((rows * length, LANE), BF16)],
        flops=rows * 2 * length * length * HEAD_DIM * 4,
    )


def second_body(
    mp_size, me_ref, x_ref, n_ref, s1_ref, par_ref, wo_ref, wg_ref, wu_ref, wd_ref, *refs
):
    t_refs = refs[:mp_size]
    att_ref, mid_ref, n2_ref, s2_ref, act_ref, slope_ref, out_ref = refs[mp_size:]
    me_m = me_ref[0]
    for mx in range(mp_size):
        m = jnp.bitwise_xor(me_m, mx)
        att_ref[:, pl.ds(col(m * LANE), LANE)] = t_refs[mx][...]
    mid = (
        x_ref[...].astype(F32)
        + nt(att_ref[...], wo_ref[...])
        + s1_ref[...] * n_ref[...].astype(F32)
    )
    mid_ref[...] = mid
    xhat, _ = norm_parts(mid)
    n2_ref[...] = (xhat * par_ref[1:2] + par_ref[4:5]).astype(BF16)
    s2_ref[...] = sigmoid(nn(n2_ref[...], wg_ref[...]) + par_ref[5:6])
    step_cols = 256

    def step(j, carry):
        cols = pl.ds(pl.multiple_of(j * step_cols, step_cols), step_cols)
        hidden = nn(n2_ref[...], wu_ref[:, cols])
        square = hidden * hidden
        th = jnp.tanh(0.7978845608 * hidden * (1.0 + 0.044715 * square))
        half = 0.5 * (1.0 + th)
        act_ref[:, cols] = (hidden * half).astype(BF16)
        inner = 0.7978845608 * (1.0 + 3 * 0.044715 * square)
        slope_ref[:, cols] = (half + 0.5 * hidden * (1.0 - th * th) * inner).astype(BF16)
        return carry

    lax.fori_loop(0, wu_ref.shape[1] // step_cols, step, 0)
    for j in range(2):
        half_cols = wo_ref.shape[0] // 2
        cols = slice(j * half_cols, (j + 1) * half_cols)
        out_ref[:, cols] = (
            mid_ref[:, cols]
            + s2_ref[:, cols] * n2_ref[:, cols].astype(F32)
            + nt(act_ref[...], wd_ref[cols, :])
        )


def second(me, x, n, s1, par_t, wo, wg, wu, wd, t_parts):
    rows, model = x.shape
    ff = wu.shape[1]
    out = [
        sds((rows, model), BF16),
        sds((rows, model), F32),
        sds((rows, model), BF16),
        sds((rows, model), F32),
        sds((rows, ff), BF16),
        sds((rows, ff), BF16),
        sds((rows, model), F32),
    ]
    return call(
        functools.partial(second_body, len(t_parts)),
        "second",
        out,
        [me, x, n, s1, par_t, wo, wg, wu, wd] + t_parts,
        smem=1,
        flops=2 * rows * (wo.size + wg.size + wu.size + wd.size),
    )


def norm_back(x, gain, d_normed):
    xhat, rstd = norm_parts(x)
    e = d_normed * gain
    mean_e = jnp.mean(e, axis=1, keepdims=True)
    mean_ex = jnp.mean(e * xhat, axis=1, keepdims=True)
    d_gain = jnp.sum(d_normed * xhat, axis=0, keepdims=True)
    d_bias = jnp.sum(d_normed, axis=0, keepdims=True)
    return (e - mean_e - xhat * mean_ex) * rstd, d_gain, d_bias


def second_back_body(
    mp_size,
    me_ref,
    g_ref,
    mid_ref,
    n2_ref,
    s2_ref,
    slope_ref,
    par_ref,
    wo_ref,
    wg_ref,
    wu_ref,
    wd_ref,
    b2_ref,
    dcomb_ref,
    gmid_ref,
    b1_ref,
    sums_ref,
    *d_refs,
):
    ff = wu_ref.shape[1]
    model = wo_ref.shape[0]
    ff_m = ff // mp_size
    stride = LANE + ff_m
    me_m = me_ref[0]
    b2_ref[...] = g_ref[...].astype(BF16)
    s2 = s2_ref[...]
    b2f = b2_ref[...].astype(F32)
    d_z2 = (b2f * n2_ref[...].astype(F32) * s2 * (1.0 - s2)).astype(BF16)
    d_n2 = b2f * s2 + nt(d_z2, wg_ref[...])
    sums_ref[2:3, :] = jnp.sum(d_z2.astype(F32), axis=0, keepdims=True)
    gmid_ref[...] = d_n2
    for m in range(mp_size):
        dcomb_ref[:, m * stride : m * stride + LANE] = d_z2[:, m * LANE : (m + 1) * LANE]
        cols = slice(m * ff_m, (m + 1) * ff_m)
        d_hidden = (nn(b2_ref[...], wd_ref[:, cols]) * slope_ref[:, cols].astype(F32)).astype(BF16)
        dcomb_ref[:, m * stride + LANE : (m + 1) * stride] = d_hidden
        gmid_ref[...] += nt(d_hidden, wu_ref[:, cols])
    d_mid, d_gain, d_bias = norm_back(mid_ref[...], par_ref[1:2], gmid_ref[...])
    sums_ref[0:1, :] = d_gain
    sums_ref[1:2, :] = d_bias
    sums_ref[3:8, :] = jnp.zeros((5, model), F32)
    g_mid = g_ref[...] + d_mid
    gmid_ref[...] = g_mid
    b1_ref[...] = g_mid.astype(BF16)
    for mx in range(mp_size):
        m = jnp.bitwise_xor(me_m, mx)
        d_refs[mx][...] = nn(b1_ref[...], wo_ref[:, pl.ds(col(m * LANE), LANE)]).astype(BF16)


def second_back(me, g, mid, n2, s2, slope, par_t, wo, wg, wu, wd, mp_size):
    rows, model = g.shape
    ff = wu.shape[1]
    out = [
        sds((rows, model), BF16),
        sds((rows, ff + LANE * mp_size), BF16),
        sds((rows, model), F32),
        sds((rows, model), BF16),
        sds((8, model), F32),
    ]
    out += [sds((rows, LANE), BF16)] * mp_size
    return call(
        functools.partial(second_back_body, mp_size),
        "second_back",
        out,
        [me, g, mid, n2, s2, slope, par_t, wo, wg, wu, wd],
        smem=1,
        flops=2 * rows * (wo.size + wg.size + wu.size + wd.size),
    )


def attend_back_body(mp_size, me_ref, seg_ref, segc_ref, segr_ref, qkv_ref, lse_ref, *refs):
    d_in = refs[:mp_size]
    d_out = refs[mp_size : 2 * mp_size]
    do_scr, dq_scr, dk_scr, dv_scr = refs[2 * mp_size :]
    rows, length = qkv_ref.shape[0], qkv_ref.shape[1]
    part = d_in[0].shape[0] // rows
    me_m = me_ref[0]
    for mx in range(mp_size):
        for r in range(rows):
            at = pl.multiple_of(r * length + jnp.bitwise_xor(me_m, mx) * part, part)
            do_scr[pl.ds(at, part), :] = d_in[mx][r * part : (r + 1) * part, :]
    dq_scr[...] = jnp.zeros_like(dq_scr)
    dk_scr[...] = jnp.zeros_like(dk_scr)
    dv_scr[...] = jnp.zeros_like(dv_scr)
    q_spans = length // SPAN

    def step(i, carry):
        r, q_at = i // q_spans, i % q_spans
        low = seg_bounds(seg_ref, r, q_at, q_spans)
        real = seg_ref[r, q_at * SPAN] >= 0
        q0 = pl.multiple_of(q_at * SPAN, SPAN)
        k0 = pl.multiple_of(low * SPAN, SPAN)
        q_abs = pl.multiple_of(i * SPAN, SPAN)
        k_abs = pl.multiple_of(r * length + low * SPAN, SPAN)
        for spans in range(1, q_spans + 1):

            @pl.when(real & (q_at - low + 1 == spans))
            def _():
                keys = spans * SPAN
                mask = allowed_t(segc_ref, segr_ref, r, k0, q0, spans)
                dqs, dks, dvs = [], [], []
                for h in range(2):
                    lo = h * HEAD_DIM
                    q = qkv_ref[r, pl.ds(q0, SPAN), lo : lo + HEAD_DIM] * jnp.asarray(
                        HEAD_DIM**-0.5, BF16
                    )
                    k = qkv_ref[r, pl.ds(k0, keys), 128 + lo : 128 + lo + HEAD_DIM]
                    v = qkv_ref[r, pl.ds(k0, keys), 256 + lo : 256 + lo + HEAD_DIM]
                    do = do_scr[pl.ds(q_abs, SPAN), lo : lo + HEAD_DIM]
                    lse = lse_ref[r * 2 + h, :, pl.ds(q0, SPAN)]
                    p = jnp.where(mask, jnp.exp(nt(k, q) - lse), 0.0)
                    dvs.append(nn(p.astype(BF16), do))
                    dp = nt(v, do)
                    delta = jnp.sum(p * dp, axis=0, keepdims=True)
                    ds = (p * (dp - delta)).astype(BF16)
                    dks.append(nn(ds, q))
                    dqs.append(tn(k, ds))
                dq_scr[pl.ds(q_abs, SPAN), :] = (
                    jnp.concatenate(dqs, axis=0).T * HEAD_DIM**-0.5
                ).astype(BF16)
                dk_scr[pl.ds(k_abs, keys), :] += jnp.concatenate(dks, axis=1)
                dv_scr[pl.ds(k_abs, keys), :] += jnp.concatenate(dvs, axis=1)

        return carry

    lax.fori_loop(0, rows * q_spans, step, 0)
    for mx in range(mp_size):
        for r in range(rows):
            at = pl.multiple_of(r * length + jnp.bitwise_xor(me_m, mx) * part, part)
            here = slice(r * part, (r + 1) * part)
            d_out[mx][here, 0:128] = dq_scr[pl.ds(at, part), :]
            d_out[mx][here, 128:256] = dk_scr[pl.ds(at, part), :].astype(BF16)
            d_out[mx][here, 256:384] = dv_scr[pl.ds(at, part), :].astype(BF16)


def attend_back(me, seg, segc, segr, qkv, lse, d_parts):
    mp_size = len(d_parts)
    rows, length = seg.shape
    local = d_parts[0].shape[0]
    return call(
        functools.partial(attend_back_body, mp_size),
        "attend_back",
        [sds((local, 384), BF16)] * mp_size,
        [me, seg, segc, segr, qkv, lse] + d_parts,
        smem=2,
        scratch=[
            pltpu.VMEM((rows * length, LANE), BF16),
            pltpu.VMEM((rows * length, LANE), BF16),
            pltpu.VMEM((rows * length, LANE), F32),
            pltpu.VMEM((rows * length, LANE), F32),
        ],
        flops=rows * 2 * length * length * HEAD_DIM * 10,
    )


def first_back_body(
    mp_size, me_ref, x_ref, gmid_ref, n_ref, s1_ref, par_ref, sums2_ref, wq_ref, *refs
):
    d_refs = refs[:mp_size]
    dcomb_ref, g_ref, sums_ref = refs[mp_size:]
    me_m = me_ref[0]
    gmid = gmid_ref[...]
    b1f = gmid.astype(BF16).astype(F32)
    s1 = s1_ref[...]
    d_z1 = (b1f * n_ref[...].astype(F32) * s1 * (1.0 - s1)).astype(BF16)
    for m in range(mp_size):
        dcomb_ref[:, m * 512 + 384 : (m + 1) * 512] = d_z1[:, m * LANE : (m + 1) * LANE]
    for mx in range(mp_size):
        m = jnp.bitwise_xor(me_m, mx)
        dcomb_ref[:, pl.ds(col(m * 512), 384)] = d_refs[mx][...]
    d_n = b1f * s1 + nt(dcomb_ref[...], wq_ref[...])
    d_x, d_gain, d_bias = norm_back(x_ref[...].astype(F32), par_ref[0:1], d_n)
    g_ref[...] = gmid + d_x
    sums_ref[0:1, :] = d_gain
    sums_ref[1:2, :] = sums2_ref[0:1, :]
    sums_ref[2:3, :] = d_bias
    sums_ref[3:4, :] = jnp.sum(d_z1.astype(F32), axis=0, keepdims=True)
    sums_ref[4:5, :] = sums2_ref[1:2, :]
    sums_ref[5:6, :] = sums2_ref[2:3, :]
    sums_ref[6:8, :] = sums2_ref[6:8, :]


def first_back(me, x, gmid, n, s1, par_t, sums2, wq, d_parts):
    rows, model = x.shape
    out = [sds((rows, wq.shape[1]), BF16), sds((rows, model), F32), sds((8, model), F32)]
    return call(
        functools.partial(first_back_body, len(d_parts)),
        "first_back",
        out,
        [me, x, gmid, n, s1, par_t, sums2, wq] + d_parts,
        smem=1,
        flops=2 * rows * wq.size,
    )


def pack_grad_body(mp_size, chunks, left_of, columns, has_sums, me_ref, *refs):
    lefts = sorted(set(left_of))
    ins, refs = refs[: len(lefts)], refs[len(lefts) :]
    rights = refs[: len(columns)]
    refs = refs[len(columns) :]
    if has_sums:
        sums_ref, refs = refs[0], refs[1:]
    outs, scr = refs[:2], refs[2:]
    model = ins[0].shape[1]
    per = model // chunks
    me_m, me_d = me_ref[0], me_ref[1]
    half = mp_size // 2
    turn = scr[0]

    def ordered(values, dst):
        if chunks == 1:
            dst[...] = values
            return
        turn[:, : values.shape[1]] = values.astype(F32)
        for dx in range(chunks):
            at = pl.multiple_of(jnp.bitwise_xor(me_d, dx) * per, per)
            dst[dx * per : (dx + 1) * per, :] = turn[pl.ds(at, per), : values.shape[1]].astype(
                dst.dtype
            )

    for i, left in enumerate(ins):
        ordered(left[...].T, scr[1 + i])
    for mx in range(mp_size):
        m = jnp.bitwise_xor(me_m, mx)
        out = outs[mx % 2]
        at_block = 0
        for left, right, (stride, offset, width) in zip(left_of, rights, columns):
            res = nn(
                scr[1 + lefts.index(left)][...],
                right[:, pl.ds(col(m * stride + offset), width)],
            ).astype(BF16)
            for b in range(width // LANE):
                for dx in range(chunks):
                    out[mx // 2, dx, (at_block + b) * per : (at_block + b + 1) * per, :] = res[
                        dx * per : (dx + 1) * per, b * LANE : (b + 1) * LANE
                    ]
            at_block += width // LANE
    if has_sums:
        flat = jnp.concatenate([sums_ref[...], jnp.zeros((LANE - 8, model), F32)], axis=0).T
        last = scr[-1]
        ordered(flat, last)
        for mx in range(mp_size):
            for dx in range(chunks):
                outs[mx % 2][mx // 2, dx, at_block * per : (at_block + 1) * per, :] = last[
                    dx * per : (dx + 1) * per, :
                ].astype(BF16)


def pack_grad(me, mp_size, chunks, lefts, left_of, rights, columns, sums=None):
    rows, model = lefts[0].shape
    per = model // chunks
    blocks = sum(c[2] for c in columns) // LANE + (sums is not None)
    scratch = [pltpu.VMEM((model, model), F32)]
    scratch += [pltpu.VMEM((model, rows), BF16)] * len(lefts)
    if sums is not None:
        scratch.append(pltpu.VMEM((model, LANE), F32))
    return call(
        functools.partial(
            pack_grad_body, mp_size, chunks, left_of, columns, sums is not None
        ),
        "pack_grad",
        [sds((mp_size // 2, chunks, blocks * per, LANE), BF16)] * 2,
        [me] + lefts + rights + ([sums] if sums is not None else []),
        smem=1,
        scratch=scratch,
        flops=2 * rows * model * sum(c[2] for c in columns) * mp_size,
    )


def swap(value, axis, size, bits):
    return lax.ppermute(value, axis, [(i, i ^ bits) for i in range(size)])


def solution(mesh):
    dp_size, mp_size, width_size = (mesh.shape[a] for a in ("dp", "mp", "width"))
    all_axes = ("mp", "dp", "width")
    direct = (dp_size, mp_size, width_size) == (2, 4, 4)

    def exchange(parts):
        far3 = swap(parts[3], "mp", mp_size, 2)
        far2 = swap(parts[2], "mp", mp_size, 2)
        near = swap(parts[1], "mp", mp_size, 1)
        third = swap(far3, "mp", mp_size, 1)
        return [parts[0], near, far2, third]

    def gather_direct(shard, turn):
        steps = [shard] + [swap(shard, "width", width_size, k) for k in range(1, width_size)]
        base = jnp.stack(steps)
        got = {(0, 0): base}
        if turn:
            got[2, 0] = swap(base, "mp", mp_size, 2)
            got[0, 1] = swap(base, "dp", dp_size, 1)
            got[2, 1] = swap(got[2, 0], "dp", dp_size, 1)
        else:
            got[0, 1] = swap(base, "dp", dp_size, 1)
            got[2, 0] = swap(base, "mp", mp_size, 2)
            got[2, 1] = swap(got[0, 1], "mp", mp_size, 2)
        for m, d in list(got):
            got[m + 1, d] = swap(got[m, d], "mp", mp_size, 1)
        parts = [got[key] for key in got]
        order = [[(m, d * width_size + w) for w in range(width_size)] for m, d in got]
        return parts, order

    def scatter_direct(even, odd, turn):
        add = lambda a, b: (a.astype(F32) + b.astype(F32)).astype(BF16)
        got = swap(odd, "mp", mp_size, 1)
        shape = (2, dp_size, width_size) + even.shape[2:]
        even, got = even.reshape(shape), got.reshape(shape)
        if turn:
            even, got = jnp.swapaxes(even, 0, 1), jnp.swapaxes(got, 0, 1)
        axes = (("mp", mp_size, 2), ("dp", dp_size, 1))
        if turn:
            axes = axes[::-1]
        send = add(even[1], got[1])
        keep = add(even[0], got[0])
        got = swap(send, *axes[0])
        send = add(keep[1], got[1])
        keep = add(keep[0], got[0])
        got = swap(send, *axes[1])
        sums = [add(keep[k], got[k]) for k in range(width_size)]
        total = sums[0].astype(F32)
        for k in range(1, width_size):
            total = total + swap(sums[k], "width", width_size, k).astype(F32)
        return total

    def on_device(
        tokens, segments, cotangent, norm_gains, biases, w_qkv, w_out, w_gate, w_up, w_down
    ):
        batch, part, model = tokens.shape
        layers = w_qkv.shape[0]
        per = w_qkv.shape[1]
        chunks = model // per
        heads_cols = w_out.shape[1]
        ff_m = w_up.shape[2]
        ff_blocks = ff_m // LANE
        me_m = lax.axis_index("mp")
        me_d = lax.axis_index("dp") * width_size + lax.axis_index("width")
        me = jnp.stack([me_m, me_d]).astype(jnp.int32)
        if not direct:
            me_pack = jnp.zeros((2,), jnp.int32)
        else:
            me_pack = me

        def blocks_of(matrix):
            return jnp.swapaxes(matrix.reshape(per, -1, LANE), 0, 1).reshape(-1, LANE)

        def shards_of(l):
            params = jnp.concatenate([norm_gains[l], biases[l]], axis=0).T
            params = jnp.pad(params, ((0, 0), (0, LANE - params.shape[1])))
            return (
                jnp.concatenate(
                    [blocks_of(w_qkv[l].reshape(per, -1)), w_gate[l, 0], params], axis=0
                ),
                jnp.concatenate([w_gate[l, 1], blocks_of(w_up[l])], axis=0),
                jnp.concatenate([w_out[l].T, blocks_of(w_down[l].T)], axis=0),
            )

        def whole_weights(shard, plan, turn, offload):
            if direct and not offload:
                parts, order = gather_direct(shard, turn)
                return unpack(parts, order, plan, per, me, model, mp_size)
            full = lax.all_gather(shard, all_axes, axis=0, tiled=True)
            if direct:
                count = mp_size * chunks
                order = [[(i // chunks, i % chunks) for i in range(count)]]
                parts = [full.reshape(count, -1, LANE)]
                zero = jnp.zeros((2,), jnp.int32)
                return unpack(parts, order, plan, per, zero, model, mp_size)
            full = full.reshape(mp_size, chunks, len(plan), per, LANE)
            outs = {}
            for b, (which, stride, _) in enumerate(plan):
                outs.setdefault(which, []).append(b)
            result = []
            for which in sorted(outs):
                b = outs[which]
                if plan[b[0]][1] is None:
                    result.append(full[0, :, b[0]].reshape(model, LANE))
                else:
                    result.append(
                        jnp.transpose(full[:, :, b[0] : b[-1] + 1], (1, 3, 0, 2, 4)).reshape(
                            model, -1
                        )
                    )
            return result

        def reduce_piece(pair, turn):
            if direct:
                return scatter_direct(pair[0], pair[1], turn)
            full = jnp.stack(pair, axis=1)
            full = full.reshape(mp_size, -1, chunks, per, LANE)
            full = jnp.swapaxes(full, 1, 2).reshape(-1, LANE)
            return lax.psum_scatter(
                full.astype(F32), all_axes, scatter_dimension=0, tiled=True
            )

        pack_chunks = chunks if direct else 1
        segc = jnp.broadcast_to(segments[:, :, None], segments.shape + (LANE,))
        segr = segments[:, None, :]

        weights = []
        for l in range(layers):
            q_sh, u_sh, d_sh = shards_of(l)
            weights.append(
                (
                    whole_weights(q_sh, PLAN_Q, 0, False),
                    whole_weights(d_sh, PLAN_D, 1, False),
                    whole_weights(u_sh, PLAN_U, 0, False),
                )
            )

        x = tokens.reshape(batch * part, model)
        saved = []
        for l in range(layers):
            (wq, par), (wo, wd), (wg, wu) = weights[l]
            n, s1, par_t, *a_parts = first(me, x, par, wq, mp_size)
            a_parts = exchange(a_parts)
            qkv, lse, *o_parts = attend(me, segments, segc, segr, a_parts)
            o_parts = exchange(o_parts)
            att, mid, n2, s2, act, slope, out = second(
                me, x, n, s1, par_t, wo, wg, wu, wd, o_parts
            )
            saved.append((x, n, s1, par_t, qkv, lse, att, mid, n2, s2, act, slope))
            x = out
        output = x.reshape(batch, part, model)

        own = lax.dynamic_slice_in_dim(segments, me_m * part, part, 1)
        g = cotangent.astype(F32) * (own >= 0).astype(F32)[:, :, None]
        g = g.reshape(batch * part, model)
        reduced = [None] * layers
        for l in reversed(range(layers)):
            (wq, par), (wo, wd), (wg, wu) = weights[l]
            x, n, s1, par_t, qkv, lse, att, mid, n2, s2, act, slope = saved[l]
            b2, dcomb, gmid, b1, sums2, *d_parts = second_back(
                me, g, mid, n2, s2, slope, par_t, wo, wg, wu, wd, mp_size
            )
            d_parts = exchange(d_parts)
            stride = LANE + ff_m
            up_grad = pack_grad(
                me_pack, mp_size, pack_chunks, [n2], [0], [dcomb], [(stride, 0, stride)]
            )
            up_sum = reduce_piece(up_grad, 0)
            down_grad = pack_grad(
                me_pack,
                mp_size,
                pack_chunks,
                [b1, b2],
                [0, 1],
                [att, act],
                [(heads_cols, 0, heads_cols), (ff_m, 0, ff_m)],
            )
            down_sum = reduce_piece(down_grad, 1)
            d_parts = attend_back(me, segments, segc, segr, qkv, lse, d_parts)
            d_parts = exchange(d_parts)
            dcomb, g, sums = first_back(me, x, gmid, n, s1, par_t, sums2, wq, d_parts)
            q_grad = pack_grad(
                me_pack, mp_size, pack_chunks, [n], [0], [dcomb], [(512, 0, 512)], sums
            )
            q_sum = reduce_piece(q_grad, 0)
            reduced[l] = (q_sum, up_sum, down_sum)
        d_tokens = g.reshape(batch, part, model)

        def unblocks(rows, count):
            return jnp.swapaxes(rows.reshape(count, per, LANE), 0, 1).reshape(per, count * LANE)

        grads = []
        for q_sum, up_sum, down_sum in reduced:
            params = q_sum[4 * per :, :6].T
            grads.append(
                (
                    params[0:2],
                    params[2::2],
                    params[3::2],
                    unblocks(q_sum[: 3 * per], 3).reshape(per, 3, LANE),
                    down_sum[:per].T,
                    jnp.stack([q_sum[3 * per : 4 * per], up_sum[:per]]),
                    unblocks(up_sum[per:], ff_blocks),
                    unblocks(down_sum[per:], ff_blocks).T,
                )
            )
        stacked = [jnp.stack([grads[l][i] for l in range(layers)]) for i in range(8)]
        return (output, d_tokens, *stacked)

    placed = (
        P(("dp", "width"), "mp", None),
        P(("dp", "width"), None),
        P(("dp", "width"), "mp", None),
        P(None, None, ("dp", "width")),
        P(None, None, ("dp", "width")),
        P(None, ("dp", "width"), None, "mp"),
        P(None, "mp", ("dp", "width")),
        P(None, None, ("dp", "width"), "mp"),
        P(None, ("dp", "width"), "mp"),
        P(None, "mp", ("dp", "width")),
    )
    return jax.shard_map(
        on_device,
        mesh=mesh,
        in_specs=placed,
        out_specs=(
            placed[0],
            placed[0],
            placed[3],
            placed[3],
            placed[3],
            placed[5],
            placed[6],
            placed[7],
            placed[8],
            placed[9],
        ),
        check_vma=False,
    )
```

time: 2110 us -> 481 us (0.23)
  waiting for transfers between devices: 1260 us -> 139 us
  blocking collectives: 457 us -> 0 us
  matrix products: 176 us -> 0 us
  Pallas kernels: 0 us -> 168 us
  starting transfers between devices: 4.24 us -> 122 us
  other arithmetic: 133 us -> 25 us
  local copies, waits for them, and re-layouts: 54 us -> 18 us
    reduce_scatter x26 -> x0, waiting for transfers between devices: 968 us -> none  [the longest x8 173 us: collect_grads(): lax.psum_scatter(branch_term.astype(jnp.bfloat16), 'mp', scatter_dimensio...]
    all_gather x14 -> x0, blocking collectives: 451 us -> none  [the longest x2 67.3 us: copy_layer(): lax.all_gather(w_down[layer_index], ('dp', 'width'), axis=1, tiled=True)]
    unnamed x50 -> x0, waiting for transfers between devices: 194 us -> none
    dot_general x120 -> x0, matrix products: 176 us -> none  [the longest x24 45 us: dot_left_t(): lax.dot_general(left_mat, right_mat, (((0,), (0,)), ((), ())), preferred_...]
    pallas_call x0 -> x24, Pallas kernels: none -> 168 us  [call(): pl.pallas_call(body, name=name, out_shape=out_shape, in_specs=specs, out_...]
    ppermute x0 -> x128, waiting for transfers between devices: none -> 139 us  [swap(): return lax.ppermute(value, axis, [(i, i ^ bits) for i in range(size)])]
    ppermute x0 -> x128, starting transfers between devices: none -> 122 us  [swap(): return lax.ppermute(value, axis, [(i, i ^ bits) for i in range(size)])]
    all_gather x16 -> x0, waiting for transfers between devices: 99.7 us -> none  [the longest x8 72.8 us: spread_grads(): return lax.all_gather(rows_bf, 'mp', axis=0, tiled=True)]
  transfers between devices with their start and end apart: 46 -> 128, of which waited for: 37 -> 35; matrix products, arithmetic and copies ran while one was open for 10% -> 6% of each run, Pallas kernels for 0% -> 31%
where the time goes in v1:
time: 481 us; the launch traced here: 475 us
  Pallas kernels  168 us (35%)
  waiting for transfers between devices  139 us (29%)
  starting transfers between devices  122 us (25%)
  other arithmetic  25 us (5%)
  local copies, waits for them, and re-layouts  18 us (4%)
    pallas_call x24, Pallas kernels, call(): pl.pallas_call(body, name=name, out_shape=out_shape, in_specs=specs, out_...  168 us
    ppermute x128, waiting for transfers between devices, swap(): return lax.ppermute(value, axis, [(i, i ^ bits) for i in range(size)])  139 us
    ppermute x128, starting transfers between devices, swap(): return lax.ppermute(value, axis, [(i, i ^ bits) for i in range(size)])  122 us
    convert_element_type x18, other arithmetic, scatter_direct(): add = lambda a, b: (a.astype(F32) + b.astype(F32)).astype(BF16)  12.9 us
  transfers between devices with their start and end apart: 128, of which 35 were waited for; matrix products, arithmetic and copies ran while one was open for 6% of the time, Pallas kernels for 31%

profile of v1, /device:TPU:0, one launch (start us, length us, event | category | flops | bytes accessed | tf_op | source)
XLA Modules:
  0.0 474.6 jit_solution(6432469216995744086)
XLA Ops:
  3.8 4.1 collective-permute-start.1
  11.2 2.0 collective-permute-start.11
  13.1 2.5 collective-permute-start.10
  19.0 4.2 collective-permute-done.11
  23.6 2.8 collective-permute-start.40
  28.2 5.1 %collective-permute-start.22 = (bf16[320,128]{1,0:T(8,128)(2,1)S(1)}, bf16[320,128]{1,0:T(8,128)(2,1)S(1)}, u32[]{:S(2)}, u32[]{:S(2)}) collective-permute-start(bf16[320,128]{1,0:T(8,128)(2,1)S(1)} %get-tuple-element.257), channel_id=1, source_target_pairs={{0,3},{1,2},{2,1},{3,0},{4,7},{5,6},{6,5},{7,4},{8,11},{9,10},{10,... | collective-permute-start | bytes 245768 | tf_op jit(solution)/shard_map/ppermute | solution.py:568
  38.2 5.3 %collective-permute-done.49 = bf16[320,128]{1,0:T(8,128)(2,1)S(1)} collective-permute-done((bf16[320,128]{1,0:T(8,128)(2,1)S(1)}, bf16[320,128]{1,0:T(8,128)(2,1)S(1)}, u32[]{:S(2)}, u32[]{:S(2)}) %collective-permute-start.49) | collective-permute-done | bytes 81952 | tf_op jit(solution)/shard_map/ppermute | solution.py:568
  45.1 2.8 collective-permute-done.48
  49.8 4.4 collective-permute-done.50
  56.8 5.0 %collective-permute-done.13.refs_1_ = bf16[4,320,128]{2,1,0:T(8,128)(2,1)S(1)} collective-permute-done((bf16[4,320,128]{2,1,0:T(8,128)(2,1)S(1)}, bf16[4,320,128]{2,1,0:T(8,128)(2,1)S(1)}, u32[]{:S(2)}, u32[]{:S(2)}) %collective-permute-start.13) | collective-permute-done | bytes 327712 | tf_op jit(solution)/shard_map/ppermute | solution.py:568
  66.5 3.6 unpack.6
  70.8 4.5 first.2
  77.2 2.3 collective-permute-done.42.refs_2_
  83.0 5.3 %collective-permute-done.15.refs_3_ = bf16[4,320,128]{2,1,0:T(8,128)(2,1)S(1)} collective-permute-done((bf16[4,320,128]{2,1,0:T(8,128)(2,1)S(1)}, bf16[4,320,128]{2,1,0:T(8,128)(2,1)S(1)}, u32[]{:S(2)}, u32[]{:S(2)}) %collective-permute-start.15) | collective-permute-done | bytes 327712 | tf_op jit(solution)/shard_map/ppermute | solution.py:568
  90.4 4.5 collective-permute-done.25.refs_3_
  96.4 6.8 %collective-permute-done.31.refs_2_ = bf16[512,384]{1,0:T(8,128)(2,1)S(1)} collective-permute-done((bf16[512,384]{1,0:T(8,128)(2,1)}, bf16[512,384]{1,0:T(8,128)(2,1)S(1)}, u32[]{:S(2)}, u32[]{:S(2)}) %collective-permute-start.31) | collective-permute-done | bytes 393248 | tf_op jit(solution)/shard_map/ppermute | solution.py:568
  105.7 12.7 %attend.2 = (bf16[2,1024,384]{2,1,0:T(8,128)(2,1)}, f32[4,1,1024]{2,1,0:T(1,128)}, bf16[512,128]{1,0:T(8,128)(2,1)}, bf16[512,128]{1,0:T(8,128)(2,1)}, bf16[512,...) custom-call(s32[2]{0:T(128)} %pad_add_fusion.me_ref, s32[2,1024]{1,0:T(2,128)} %seg_ref.7, ...), custom_call_target="tpu_custom_call" | custom-call | flops 1073741824 | bytes 4751368 | tf_op jit(solution)/shard_map/attend/pallas_call | solution.py:40
  121.5 2.9 collective-permute-done.36
  125.4 3.9 unpack.7
  129.3 3.8 unpack.8
  133.7 2.0 collective-permute-start.58
  135.8 3.5 unpack.9
  142.8 11.5 %second.2 = (bf16[512,512]{1,0:T(8,128)(2,1)}, f32[512,512]{1,0:T(8,128)}, bf16[512,512]{1,0:T(8,128)(2,1)}, f32[512,512]{1,0:T(8,128)}, bf16[512,2048]{1,0:T(8,...) custom-call(s32[2]{0:T(128)} %pad_add_fusion.me_ref, bf16[512,512]{1,0:T(8,128)(2,1)} %bitcast.433, ...), custom_call_target="tpu_custom_call" | custom-call | flops 2684354560 | bytes 16269320 | tf_op jit(solution)/shard_map/second/pallas_call | solution.py:40
  154.3 4.8 %first.3 = (bf16[512,512]{1,0:T(8,128)(2,1)}, f32[512,512]{1,0:T(8,128)}, f32[8,512]{1,0:T(8,128)}, bf16[512,384]{1,0:T(8,128)(2,1)}, bf16[512,384]{1,0:T(8,128)...) custom-call(s32[2]{0:T(128)} %pad_add_fusion.me_ref, f32[512,512]{1,0:T(8,128)} %get-tuple-element.123.x_ref, ...), custom_call_target="tpu_custom_call" | custom-call | flops 1073741824 | bytes 6438920 | tf_op jit(solution)/shard_map/first/pallas_call | solution.py:40
  159.0 2.3 collective-permute-start.51
  161.6 2.0 collective-permute-start.62
  163.8 6.1 %collective-permute-done.51.refs_1_ = bf16[4,320,128]{2,1,0:T(8,128)(2,1)S(1)} collective-permute-done((bf16[4,320,128]{2,1,0:T(8,128)(2,1)S(1)}, bf16[4,320,128]{2,1,0:T(8,128)(2,1)S(1)}, u32[]{:S(2)}, u32[]{:S(2)}) %collective-permute-start.51) | collective-permute-done | bytes 327712 | tf_op jit(solution)/shard_map/ppermute | solution.py:568
  171.9 12.9 %collective-permute-done.62.refs_2_ = bf16[4,320,128]{2,1,0:T(8,128)(2,1)S(1)} collective-permute-done((bf16[4,320,128]{2,1,0:T(8,128)(2,1)S(1)}, bf16[4,320,128]{2,1,0:T(8,128)(2,1)S(1)}, u32[]{:S(2)}, u32[]{:S(2)}) %collective-permute-start.62) | collective-permute-done | bytes 327712 | tf_op jit(solution)/shard_map/ppermute | solution.py:568
  187.5 9.6 %collective-permute-done.69.refs_2_ = bf16[512,384]{1,0:T(8,128)(2,1)S(1)} collective-permute-done((bf16[512,384]{1,0:T(8,128)(2,1)}, bf16[512,384]{1,0:T(8,128)(2,1)S(1)}, u32[]{:S(2)}, u32[]{:S(2)}) %collective-permute-start.69) | collective-permute-done | bytes 393248 | tf_op jit(solution)/shard_map/ppermute | solution.py:568
  198.0 12.4 %attend.3 = (bf16[2,1024,384]{2,1,0:T(8,128)(2,1)}, f32[4,1,1024]{2,1,0:T(1,128)}, bf16[512,128]{1,0:T(8,128)(2,1)}, bf16[512,128]{1,0:T(8,128)(2,1)}, bf16[512,...) custom-call(s32[2]{0:T(128)} %pad_add_fusion.me_ref, s32[2,1024]{1,0:T(2,128)} %seg_ref.7, ...), custom_call_target="tpu_custom_call" | custom-call | flops 1073741824 | bytes 4751368 | tf_op jit(solution)/shard_map/attend/pallas_call | solution.py:40
  214.0 2.6 collective-permute-done.74
  217.7 3.7 unpack.10
  222.9 3.8 unpack.11
  227.5 11.7 %second.3 = (bf16[512,512]{1,0:T(8,128)(2,1)}, f32[512,512]{1,0:T(8,128)}, bf16[512,512]{1,0:T(8,128)(2,1)}, f32[512,512]{1,0:T(8,128)}, bf16[512,2048]{1,0:T(8,...) custom-call(s32[2]{0:T(128)} %pad_add_fusion.me_ref, f32[512,512]{1,0:T(8,128)} %get-tuple-element.123.x_ref, ...), custom_call_target="tpu_custom_call" | custom-call | flops 2684354560 | bytes 16793608 | tf_op jit(solution)/shard_map/second/pallas_call | solution.py:40
  239.1 8.9 %second_back.2 = (bf16[512,512]{1,0:T(8,128)(2,1)}, bf16[512,2560]{1,0:T(8,128)(2,1)}, f32[512,512]{1,0:T(8,128)}, bf16[512,512]{1,0:T(8,128)(2,1)}, f32[8,512]{...) custom-call(s32[2]{0:T(128)} %pad_add_fusion.me_ref, ...), custom_call_target="tpu_custom_call" | custom-call | flops 2684354560 | bytes 16285704 | tf_op jit(solution)/shard_map/second_back/pallas_call | solution.py:40
  248.1 2.3 collective-permute-start.78
  251.0 4.0 collective-permute-done.78
  254.9 5.2 %pack_grad.11 = (bf16[2,8,320,128]{3,2,1,0:T(8,128)(2,1)}, bf16[2,8,320,128]{3,2,1,0:T(8,128)(2,1)}) custom-call(s32[2]{0:T(128)} %pad_add_fusion.me_ref, bf16[512,512]{1,0:T(8,128)(2,1)} %get-tuple-element.143.n2_ref.refs_0_, bf16[512,2560]{1,0:T(8,128)(2,1)} %get-tuple-element.199.refs_1_), custom_call_target="tpu_custom_call" | custom-call | flops 1342177280 | bytes 5767176 | tf_op jit(solution)/shard_map/pack_grad/pallas_call | solution.py:40
  261.4 13.7 %attend_back.2 = (bf16[512,384]{1,0:T(8,128)(2,1)}, bf16[512,384]{1,0:T(8,128)(2,1)}, bf16[512,384]{1,0:T(8,128)(2,1)}, bf16[512,384]{1,0:T(8,128)(2,1)}) custom-call(s32[2]{0:T(128)} %pad_add_fusion.me_ref, s32[2,1024]{1,0:T(2,128)} %seg_ref.7, s32[2,1024,128]{2,1,0:T(8,128)} %broadcast_in_dim.4.segc_ref, s32[2,1,1024]{2,1,0:T(1,128)} %broadcast_in_dim.5.segr_ref, ...), custom_call_target="tpu_custom_call" | custom-call | flops 2684354560 | bytes 4751368 | tf_op jit(solution)/shard_map/attend_back/pallas_call | solution.py:40
  277.0 5.5 %pack_grad.9 = (bf16[2,8,320,128]{3,2,1,0:T(8,128)(2,1)}, bf16[2,8,320,128]{3,2,1,0:T(8,128)(2,1)}) custom-call(s32[2]{0:T(128)} %pad_add_fusion.me_ref, bf16[512,512]{1,0:T(8,128)(2,1)} %get-tuple-element.190.refs_0_, bf16[512,512]{1,0:T(8,128)(2,1)} %get-tuple-element.191.refs_1_, bf16[512,512]{1,0:T(8,128)(2,1)} %get-tuple-element.192.refs_2_, ...), custom_call_target="tpu_custom_call" | custom-call | flops 1342177280 | bytes 6291464 | tf_op jit(solution)/shard_map/pack_grad/pallas_call | solution.py:40
  283.1 4.1 collective-permute-done.82
  287.3 7.7 %collective-permute-done.81.refs_2_ = bf16[512,384]{1,0:T(8,128)(2,1)S(1)} collective-permute-done((bf16[512,384]{1,0:T(8,128)(2,1)S(1)}, bf16[512,384]{1,0:T(8,128)(2,1)S(1)}, u32[]{:S(2)}, u32[]{:S(2)}) %collective-permute-start.81) | collective-permute-done | bytes 393248 | tf_op jit(solution)/shard_map/ppermute | solution.py:568
  295.9 6.7 %first_back.2 = (bf16[512,2048]{1,0:T(8,128)(2,1)}, f32[512,512]{1,0:T(8,128)}, f32[8,512]{1,0:T(8,128)}) custom-call(s32[2]{0:T(128)} %pad_add_fusion.me_ref, f32[512,512]{1,0:T(8,128)} %get-tuple-element.123.x_ref, f32[512,512]{1,0:T(8,128)} %get-tuple-element.146.gmid_ref, bf16[512,512]{1,0:T(8,128)(2,1)} %get-tuple-element.126.n_ref.refs_0_, ...), custom_call_target="tpu_custom_call" | custom-call | flops 1073741824 | bytes 10534920 | tf_op jit(solution)/shard_map/first_back/pallas_call | solution.py:40
  302.5 9.0 %second_back.3 = (bf16[512,512]{1,0:T(8,128)(2,1)}, bf16[512,2560]{1,0:T(8,128)(2,1)}, f32[512,512]{1,0:T(8,128)}, bf16[512,512]{1,0:T(8,128)(2,1)}, f32[8,512]{...) custom-call(s32[2]{0:T(128)} %pad_add_fusion.me_ref, ...), custom_call_target="tpu_custom_call" | custom-call | flops 2684354560 | bytes 16285704 | tf_op jit(solution)/shard_map/second_back/pallas_call | solution.py:40
  314.5 2.5 collective-permute-done.86
  318.3 2.4 collective-permute-start.123
  321.5 13.4 %attend_back.3 = (bf16[512,384]{1,0:T(8,128)(2,1)}, bf16[512,384]{1,0:T(8,128)(2,1)}, bf16[512,384]{1,0:T(8,128)(2,1)}, bf16[512,384]{1,0:T(8,128)(2,1)}) custom-call(s32[2]{0:T(128)} %pad_add_fusion.me_ref, s32[2,1024]{1,0:T(2,128)} %seg_ref.7, s32[2,1024,128]{2,1,0:T(8,128)} %broadcast_in_dim.4.segc_ref, s32[2,1,1024]{2,1,0:T(1,128)} %broadcast_in_dim.5.segr_ref, ...), custom_call_target="tpu_custom_call" | custom-call | flops 2684354560 | bytes 4751368 | tf_op jit(solution)/shard_map/attend_back/pallas_call | solution.py:40
  339.2 5.4 %pack_grad.8 = (bf16[2,8,320,128]{3,2,1,0:T(8,128)(2,1)}, bf16[2,8,320,128]{3,2,1,0:T(8,128)(2,1)}) custom-call(s32[2]{0:T(128)} %pad_add_fusion.me_ref, bf16[512,512]{1,0:T(8,128)(2,1)} %get-tuple-element.184.refs_0_, bf16[512,512]{1,0:T(8,128)(2,1)} %get-tuple-element.185.refs_1_, bf16[512,512]{1,0:T(8,128)(2,1)} %get-tuple-element.186.refs_2_, ...), custom_call_target="tpu_custom_call" | custom-call | flops 1342177280 | bytes 6291464 | tf_op jit(solution)/shard_map/pack_grad/pallas_call | solution.py:40
  344.8 5.2 %pack_grad.10 = (bf16[2,8,320,128]{3,2,1,0:T(8,128)(2,1)}, bf16[2,8,320,128]{3,2,1,0:T(8,128)(2,1)}) custom-call(s32[2]{0:T(128)} %pad_add_fusion.me_ref, bf16[512,512]{1,0:T(8,128)(2,1)} %get-tuple-element.160.n2_ref.refs_0_, bf16[512,2560]{1,0:T(8,128)(2,1)} %get-tuple-element.196.refs_1_), custom_call_target="tpu_custom_call" | custom-call | flops 1342177280 | bytes 5767176 | tf_op jit(solution)/shard_map/pack_grad/pallas_call | solution.py:40
  350.6 4.4 pack_grad.7
  359.4 6.5 %first_back.3 = (bf16[512,2048]{1,0:T(8,128)(2,1)}, f32[512,512]{1,0:T(8,128)}, f32[8,512]{1,0:T(8,128)}) custom-call(s32[2]{0:T(128)} %pad_add_fusion.me_ref, bf16[512,512]{1,0:T(8,128)(2,1)} %bitcast.434, f32[512,512]{1,0:T(8,128)} %get-tuple-element.163.gmid_ref, bf16[512,512]{1,0:T(8,128)(2,1)} %get-tuple-element.108.n_ref.refs_0_, ...), custom_call_target="tpu_custom_call" | custom-call | flops 1073741824 | bytes 10010632 | tf_op jit(solution)/shard_map/first_back/pallas_call | solution.py:40
  365.9 4.5 pack_grad.6
  371.7 2.0 collective-permute-start.127
  375.5 2.6 add_convert_fusion.3
  379.1 2.5 add_convert_fusion.9
  394.9 8.6 %collective-permute-done.117 = bf16[2,4,320,128]{3,2,1,0:T(8,128)(2,1)} collective-permute-done((bf16[2,4,320,128]{3,2,1,0:T(8,128)(2,1)}, bf16[2,4,320,128]{3,2,1,0:T(8,128)(2,1)}, u32[]{:S(2)}, u32[]{:S(2)}) %collective-permute-start.117) | collective-permute-done | bytes 655392 | tf_op jit(solution)/shard_map/ppermute | solution.py:568
  408.0 9.4 %collective-permute-done.99 = bf16[2,4,320,128]{3,2,1,0:T(8,128)(2,1)S(1)} collective-permute-done((bf16[2,4,320,128]{3,2,1,0:T(8,128)(2,1)}, bf16[2,4,320,128]{3,2,1,0:T(8,128)(2,1)S(1)}, u32[]{:S(2)}, u32[]{:S(2)}) %collective-permute-start.99) | collective-permute-done | bytes 655392 | tf_op jit(solution)/shard_map/ppermute | solution.py:568
  418.8 2.1 collective-permute-start.119
  429.2 2.1 collective-permute-start.103
  438.2 4.2 collective-permute-done.102
  446.2 2.9 collective-permute-done.93
  450.4 6.0 %collective-permute-done.94 = bf16[4,320,128]{2,1,0:T(8,128)(2,1)S(1)} collective-permute-done((bf16[4,320,128]{2,1,0:T(8,128)(2,1)S(1)}, bf16[4,320,128]{2,1,0:T(8,128)(2,1)S(1)}, u32[]{:S(2)}, u32[]{:S(2)}) %collective-permute-start.94) | collective-permute-done | bytes 327712 | tf_op jit(solution)/shard_map/ppermute | solution.py:568
  456.5 6.2 %collective-permute-start.95 = (bf16[320,128]{1,0:T(8,128)(2,1)S(1)}, bf16[320,128]{1,0:T(8,128)(2,1)S(1)}, u32[]{:S(2)}, u32[]{:S(2)}) collective-permute-start(bf16[320,128]{1,0:T(8,128)(2,1)S(1)} %get-tuple-element.238), channel_id=1, source_target_pairs={{0,1},{1,0},{2,3},{3,2},{4,5},{5,4},{6,7},{7,6},{8,9},{9,8},{10,11... | collective-permute-start | bytes 245768 | tf_op jit(solution)/shard_map/ppermute | solution.py:568
  466.0 3.0 collective-permute-done.97
  (495 shorter events, 131.8 us)
Async XLA Ops:
  11.2 12.1 %collective-permute-start.11 = (bf16[320,128]{1,0:T(8,128)(2,1)S(1)}, bf16[320,128]{1,0:T(8,128)(2,1)S(1)}, u32[]{:S(2)}, u32[]{:S(2)}) collective-permute-start(bf16[320,128]{1,0:T(8,128)(2,1)S(1)} %get-tuple-element.259), channel_id=1, source_target_pairs={{0,2},{1,3},{2,0},{3,1},{4,6},{5,7},{6,4},{7,5},{8,10},{9,11},{10,... | collective-permute-start | bytes 245768 | tf_op jit(solution)/shard_map/ppermute | solution.py:568
  17.4 26.0 %collective-permute-start.3 = (bf16[4,320,128]{2,1,0:T(8,128)(2,1)S(1)}, bf16[4,320,128]{2,1,0:T(8,128)(2,1)S(1)}, u32[]{:S(2)}, u32[]{:S(2)}) collective-permute-start(bf16[4,320,128]{2,1,0:T(8,128)(2,1)S(1)} %pad_maximum_fusion.refs_0_), channel_id=1, source_target_pairs={{0,16},{16,0},{1,17},{17,1},{2,18},{18,2},{3,19},{19,3},{4,20},{20... | collective-permute-start | bytes 983048 | tf_op jit(solution)/shard_map/ppermute | solution.py:568
  33.3 22.4 %collective-permute-start.4 = (bf16[4,320,128]{2,1,0:T(8,128)(2,1)S(1)}, bf16[4,320,128]{2,1,0:T(8,128)(2,1)S(1)}, u32[]{:S(2)}, u32[]{:S(2)}) collective-permute-start(bf16[4,320,128]{2,1,0:T(8,128)(2,1)S(1)} %pad_maximum_fusion.refs_0_), channel_id=1, source_target_pairs={{0,8},{4,12},{8,0},{12,4},{1,9},{5,13},{9,1},{13,5},{2,10},{6,14},... | collective-permute-start | bytes 983048 | tf_op jit(solution)/shard_map/ppermute | solution.py:568
  36.5 19.2 %collective-permute-start.16 = (bf16[4,320,128]{2,1,0:T(8,128)(2,1)S(1)}, bf16[4,320,128]{2,1,0:T(8,128)(2,1)S(1)}, u32[]{:S(2)}, u32[]{:S(2)}) collective-permute-start(bf16[4,320,128]{2,1,0:T(8,128)(2,1)S(1)} %pad_maximum_fusion.1.refs_0_), channel_id=1, source_target_pairs={{0,4},{4,0},{8,12},{12,8},{1,5},{5,1},{9,13},{13,9},{2,6},{6,2},{1... | collective-permute-start | bytes 983048 | tf_op jit(solution)/shard_map/ppermute | solution.py:568
  36.6 19.6 %collective-permute-start.14 = (bf16[4,320,128]{2,1,0:T(8,128)(2,1)S(1)}, bf16[4,320,128]{2,1,0:T(8,128)(2,1)S(1)}, u32[]{:S(2)}, u32[]{:S(2)}) collective-permute-start(bf16[4,320,128]{2,1,0:T(8,128)(2,1)S(1)} %pad_maximum_fusion.1.refs_0_), channel_id=1, source_target_pairs={{0,16},{16,0},{1,17},{17,1},{2,18},{18,2},{3,19},{19,3},{4,20},{20... | collective-permute-start | bytes 983048 | tf_op jit(solution)/shard_map/ppermute | solution.py:568
  43.5 12.8 %collective-permute-start.5 = (bf16[4,320,128]{2,1,0:T(8,128)(2,1)S(1)}, bf16[4,320,128]{2,1,0:T(8,128)(2,1)S(1)}, u32[]{:S(2)}, u32[]{:S(2)}) collective-permute-start(bf16[4,320,128]{2,1,0:T(8,128)(2,1)S(1)} %collective-permute-done.3.refs_1_), channel_id=1, source_target_pairs={{0,8},{4,12},{8,0},{12,4},{1,9},{5,13},{9,1},{13,5},{2,10},{6,14},... | collective-permute-start | bytes 983048 | tf_op jit(solution)/shard_map/ppermute | solution.py:568
  61.8 13.5 %collective-permute-start.24 = (bf16[4,320,128]{2,1,0:T(8,128)(2,1)S(1)}, bf16[4,320,128]{2,1,0:T(8,128)(2,1)S(1)}, u32[]{:S(2)}, u32[]{:S(2)}) collective-permute-start(bf16[4,320,128]{2,1,0:T(8,128)(2,1)S(1)} %pad_maximum_fusion.2.refs_0_), channel_id=1, source_target_pairs={{0,8},{4,12},{8,0},{12,4},{1,9},{5,13},{9,1},{13,5},{2,10},{6,14},... | collective-permute-start | bytes 983048 | tf_op jit(solution)/shard_map/ppermute | solution.py:568
  63.4 13.3 %collective-permute-start.23 = (bf16[4,320,128]{2,1,0:T(8,128)(2,1)S(1)}, bf16[4,320,128]{2,1,0:T(8,128)(2,1)}, u32[]{:S(2)}, u32[]{:S(2)}) collective-permute-start(bf16[4,320,128]{2,1,0:T(8,128)(2,1)S(1)} %pad_maximum_fusion.2.refs_0_), channel_id=1, source_target_pairs={{0,16},{16,0},{1,17},{17,1},{2,18},{18,2},{3,19},{19,3},{4,20},{20... | collective-permute-start | bytes 983048 | tf_op jit(solution)/shard_map/ppermute | solution.py:568
  65.1 14.4 %collective-permute-start.42 = (bf16[4,320,128]{2,1,0:T(8,128)(2,1)S(1)}, bf16[4,320,128]{2,1,0:T(8,128)(2,1)}, u32[]{:S(2)}, u32[]{:S(2)}) collective-permute-start(bf16[4,320,128]{2,1,0:T(8,128)(2,1)S(1)} %pad_maximum_fusion.3.refs_0_), channel_id=1, source_target_pairs={{0,8},{4,12},{8,0},{12,4},{1,9},{5,13},{9,1},{13,5},{2,10},{6,14},... | collective-permute-start | bytes 983048 | tf_op jit(solution)/shard_map/ppermute | solution.py:568
  75.3 14.6 %collective-permute-start.32 = (bf16[512,384]{1,0:T(8,128)(2,1)}, bf16[512,384]{1,0:T(8,128)(2,1)S(1)}, u32[]{:S(2)}, u32[]{:S(2)}) collective-permute-start(bf16[512,384]{1,0:T(8,128)(2,1)} %get-tuple-element.118), channel_id=1, source_target_pairs={{0,8},{4,12},{8,0},{12,4},{1,9},{5,13},{9,1},{13,5},{2,10},{6,14},... | collective-permute-start | bytes 1179656 | tf_op jit(solution)/shard_map/ppermute | solution.py:568
  81.0 13.8 %collective-permute-start.30 = (bf16[512,384]{1,0:T(8,128)(2,1)}, bf16[512,384]{1,0:T(8,128)(2,1)S(1)}, u32[]{:S(2)}, u32[]{:S(2)}) collective-permute-start(bf16[512,384]{1,0:T(8,128)(2,1)} %get-tuple-element.116), channel_id=1, source_target_pairs={{0,4},{4,0},{8,12},{12,8},{1,5},{5,1},{9,13},{13,9},{2,6},{6,2},{1... | collective-permute-start | bytes 1179656 | tf_op jit(solution)/shard_map/ppermute | solution.py:568
  81.5 13.3 %collective-permute-start.25 = (bf16[4,320,128]{2,1,0:T(8,128)(2,1)}, bf16[4,320,128]{2,1,0:T(8,128)(2,1)S(1)}, u32[]{:S(2)}, u32[]{:S(2)}) collective-permute-start(bf16[4,320,128]{2,1,0:T(8,128)(2,1)} %collective-permute-done.23.refs_1_), channel_id=1, source_target_pairs={{0,8},{4,12},{8,0},{12,4},{1,9},{5,13},{9,1},{13,5},{2,10},{6,14},... | collective-permute-start | bytes 983048 | tf_op jit(solution)/shard_map/ppermute | solution.py:568
  88.3 14.9 %collective-permute-start.31 = (bf16[512,384]{1,0:T(8,128)(2,1)}, bf16[512,384]{1,0:T(8,128)(2,1)S(1)}, u32[]{:S(2)}, u32[]{:S(2)}) collective-permute-start(bf16[512,384]{1,0:T(8,128)(2,1)} %get-tuple-element.117), channel_id=1, source_target_pairs={{0,8},{4,12},{8,0},{12,4},{1,9},{5,13},{9,1},{13,5},{2,10},{6,14},... | collective-permute-start | bytes 1179656 | tf_op jit(solution)/shard_map/ppermute | solution.py:568
  89.9 13.4 %collective-permute-start.33 = (bf16[512,384]{1,0:T(8,128)(2,1)S(1)}, bf16[512,384]{1,0:T(8,128)(2,1)S(1)}, u32[]{:S(2)}, u32[]{:S(2)}) collective-permute-start(bf16[512,384]{1,0:T(8,128)(2,1)S(1)} %collective-permute-done.32), channel_id=1, source_target_pairs={{0,4},{4,0},{8,12},{12,8},{1,5},{5,1},{9,13},{13,9},{2,6},{6,2},{1... | collective-permute-start | bytes 1179656 | tf_op jit(solution)/shard_map/ppermute | solution.py:568
  89.9 28.6 %collective-permute-start.27 = (bf16[4,320,128]{2,1,0:T(8,128)(2,1)}, bf16[4,320,128]{2,1,0:T(8,128)(2,1)S(1)}, u32[]{:S(2)}, u32[]{:S(2)}) collective-permute-start(bf16[4,320,128]{2,1,0:T(8,128)(2,1)} %collective-permute-done.23.refs_1_), channel_id=1, source_target_pairs={{0,4},{4,0},{8,12},{12,8},{1,5},{5,1},{9,13},{13,9},{2,6},{6,2},{1... | collective-permute-start | bytes 983048 | tf_op jit(solution)/shard_map/ppermute | solution.py:568
  94.8 25.3 %collective-permute-start.46 = (bf16[4,320,128]{2,1,0:T(8,128)(2,1)}, bf16[4,320,128]{2,1,0:T(8,128)(2,1)S(1)}, u32[]{:S(2)}, u32[]{:S(2)}) collective-permute-start(bf16[4,320,128]{2,1,0:T(8,128)(2,1)} %collective-permute-done.42.refs_2_), channel_id=1, source_target_pairs={{0,4},{4,0},{8,12},{12,8},{1,5},{5,1},{9,13},{13,9},{2,6},{6,2},{1... | collective-permute-start | bytes 983048 | tf_op jit(solution)/shard_map/ppermute | solution.py:568
  94.9 25.3 %collective-permute-start.43 = (bf16[4,320,128]{2,1,0:T(8,128)(2,1)S(1)}, bf16[4,320,128]{2,1,0:T(8,128)(2,1)S(1)}, u32[]{:S(2)}, u32[]{:S(2)}) collective-permute-start(bf16[4,320,128]{2,1,0:T(8,128)(2,1)S(1)} %collective-permute-done.41.refs_1_), channel_id=1, source_target_pairs={{0,8},{4,12},{8,0},{12,4},{1,9},{5,13},{9,1},{13,5},{2,10},{6,14},... | collective-permute-start | bytes 983048 | tf_op jit(solution)/shard_map/ppermute | solution.py:568
  103.3 17.5 %collective-permute-start.19 = (bf16[4,320,128]{2,1,0:T(8,128)(2,1)S(1)}, bf16[4,320,128]{2,1,0:T(8,128)(2,1)}, u32[]{:S(2)}, u32[]{:S(2)}) collective-permute-start(bf16[4,320,128]{2,1,0:T(8,128)(2,1)S(1)} %collective-permute-done.15.refs_3_), channel_id=1, source_target_pairs={{0,4},{4,0},{8,12},{12,8},{1,5},{5,1},{9,13},{13,9},{2,6},{6,2},{1... | collective-permute-start | bytes 983048 | tf_op jit(solution)/shard_map/ppermute | solution.py:568
  103.3 17.6 %collective-permute-start.29 = (bf16[4,320,128]{2,1,0:T(8,128)(2,1)S(1)}, bf16[4,320,128]{2,1,0:T(8,128)(2,1)}, u32[]{:S(2)}, u32[]{:S(2)}) collective-permute-start(bf16[4,320,128]{2,1,0:T(8,128)(2,1)S(1)} %collective-permute-done.25.refs_3_), channel_id=1, source_target_pairs={{0,4},{4,0},{8,12},{12,8},{1,5},{5,1},{9,13},{13,9},{2,6},{6,2},{1... | collective-permute-start | bytes 983048 | tf_op jit(solution)/shard_map/ppermute | solution.py:568
  120.1 13.0 %collective-permute-start.45 = (bf16[4,320,128]{2,1,0:T(8,128)(2,1)S(1)}, bf16[4,320,128]{2,1,0:T(8,128)(2,1)S(1)}, u32[]{:S(2)}, u32[]{:S(2)}) collective-permute-start(bf16[4,320,128]{2,1,0:T(8,128)(2,1)S(1)} %collective-permute-done.41.refs_1_), channel_id=1, source_target_pairs={{0,4},{4,0},{8,12},{12,8},{1,5},{5,1},{9,13},{13,9},{2,6},{6,2},{1... | collective-permute-start | bytes 983048 | tf_op jit(solution)/shard_map/ppermute | solution.py:568
  120.2 13.5 %collective-permute-start.47 = (bf16[4,320,128]{2,1,0:T(8,128)(2,1)S(1)}, bf16[4,320,128]{2,1,0:T(8,128)(2,1)S(1)}, u32[]{:S(2)}, u32[]{:S(2)}) collective-permute-start(bf16[4,320,128]{2,1,0:T(8,128)(2,1)S(1)} %collective-permute-done.43.refs_3_), channel_id=1, source_target_pairs={{0,4},{4,0},{8,12},{12,8},{1,5},{5,1},{9,13},{13,9},{2,6},{6,2},{1... | collective-permute-start | bytes 983048 | tf_op jit(solution)/shard_map/ppermute | solution.py:568
  120.8 18.5 %collective-permute-start.34 = (bf16[512,128]{1,0:T(8,128)(2,1)}, bf16[512,128]{1,0:T(8,128)(2,1)S(1)}, u32[]{:S(2)}, u32[]{:S(2)}) collective-permute-start(bf16[512,128]{1,0:T(8,128)(2,1)} %get-tuple-element.120), channel_id=1, source_target_pairs={{0,4},{4,0},{8,12},{12,8},{1,5},{5,1},{9,13},{13,9},{2,6},{6,2},{1... | collective-permute-start | bytes 393224 | tf_op jit(solution)/shard_map/ppermute | solution.py:568
  120.9 20.3 %collective-permute-start.35 = (bf16[512,128]{1,0:T(8,128)(2,1)}, bf16[512,128]{1,0:T(8,128)(2,1)S(1)}, u32[]{:S(2)}, u32[]{:S(2)}) collective-permute-start(bf16[512,128]{1,0:T(8,128)(2,1)} %get-tuple-element.121), channel_id=1, source_target_pairs={{0,8},{4,12},{8,0},{12,4},{1,9},{5,13},{9,1},{13,5},{2,10},{6,14},... | collective-permute-start | bytes 393224 | tf_op jit(solution)/shard_map/ppermute | solution.py:568
  124.4 16.8 %collective-permute-start.37 = (bf16[512,128]{1,0:T(8,128)(2,1)S(1)}, bf16[512,128]{1,0:T(8,128)(2,1)S(1)}, u32[]{:S(2)}, u32[]{:S(2)}) collective-permute-start(bf16[512,128]{1,0:T(8,128)(2,1)S(1)} %collective-permute-done.36), channel_id=1, source_target_pairs={{0,4},{4,0},{8,12},{12,8},{1,5},{5,1},{9,13},{13,9},{2,6},{6,2},{1... | collective-permute-start | bytes 393224 | tf_op jit(solution)/shard_map/ppermute | solution.py:568
  133.1 25.9 %collective-permute-start.59 = (bf16[320,128]{1,0:T(8,128)(2,1)S(1)}, bf16[320,128]{1,0:T(8,128)(2,1)S(1)}, u32[]{:S(2)}, u32[]{:S(2)}) collective-permute-start(bf16[320,128]{1,0:T(8,128)(2,1)S(1)} %get-tuple-element.251), channel_id=1, source_target_pairs={{0,2},{1,3},{2,0},{3,1},{4,6},{5,7},{6,4},{7,5},{8,10},{9,11},{10,... | collective-permute-start | bytes 245768 | tf_op jit(solution)/shard_map/ppermute | solution.py:568
  133.7 27.6 %collective-permute-start.58 = (bf16[320,128]{1,0:T(8,128)(2,1)S(1)}, bf16[320,128]{1,0:T(8,128)(2,1)S(1)}, u32[]{:S(2)}, u32[]{:S(2)}) collective-permute-start(bf16[320,128]{1,0:T(8,128)(2,1)S(1)} %get-tuple-element.251), channel_id=1, source_target_pairs={{0,1},{1,0},{2,3},{3,2},{4,5},{5,4},{6,7},{7,6},{8,9},{9,8},{10,11... | collective-permute-start | bytes 245768 | tf_op jit(solution)/shard_map/ppermute | solution.py:568
  139.3 22.2 %collective-permute-start.60 = (bf16[320,128]{1,0:T(8,128)(2,1)S(1)}, bf16[320,128]{1,0:T(8,128)(2,1)S(1)}, u32[]{:S(2)}, u32[]{:S(2)}) collective-permute-start(bf16[320,128]{1,0:T(8,128)(2,1)S(1)} %get-tuple-element.251), channel_id=1, source_target_pairs={{0,3},{1,2},{2,1},{3,0},{4,7},{5,6},{6,5},{7,4},{8,11},{9,10},{10,... | collective-permute-start | bytes 245768 | tf_op jit(solution)/shard_map/ppermute | solution.py:568
  141.2 20.4 %collective-permute-start.54 = (bf16[4,320,128]{2,1,0:T(8,128)(2,1)S(1)}, bf16[4,320,128]{2,1,0:T(8,128)(2,1)S(1)}, u32[]{:S(2)}, u32[]{:S(2)}) collective-permute-start(bf16[4,320,128]{2,1,0:T(8,128)(2,1)S(1)} %pad_maximum_fusion.4.refs_0_), channel_id=1, source_target_pairs={{0,4},{4,0},{8,12},{12,8},{1,5},{5,1},{9,13},{13,9},{2,6},{6,2},{1... | collective-permute-start | bytes 983048 | tf_op jit(solution)/shard_map/ppermute | solution.py:568
  141.2 22.4 %collective-permute-start.52 = (bf16[4,320,128]{2,1,0:T(8,128)(2,1)S(1)}, bf16[4,320,128]{2,1,0:T(8,128)(2,1)S(1)}, u32[]{:S(2)}, u32[]{:S(2)}) collective-permute-start(bf16[4,320,128]{2,1,0:T(8,128)(2,1)S(1)} %pad_maximum_fusion.4.refs_0_), channel_id=1, source_target_pairs={{0,16},{16,0},{1,17},{17,1},{2,18},{18,2},{3,19},{19,3},{4,20},{20... | collective-permute-start | bytes 983048 | tf_op jit(solution)/shard_map/ppermute | solution.py:568
  161.4 25.2 %collective-permute-start.70 = (bf16[512,384]{1,0:T(8,128)(2,1)}, bf16[512,384]{1,0:T(8,128)(2,1)S(1)}, u32[]{:S(2)}, u32[]{:S(2)}) collective-permute-start(bf16[512,384]{1,0:T(8,128)(2,1)} %get-tuple-element.136), channel_id=1, source_target_pairs={{0,8},{4,12},{8,0},{12,4},{1,9},{5,13},{9,1},{13,5},{2,10},{6,14},... | collective-permute-start | bytes 1179656 | tf_op jit(solution)/shard_map/ppermute | solution.py:568
  161.6 23.2 %collective-permute-start.62 = (bf16[4,320,128]{2,1,0:T(8,128)(2,1)S(1)}, bf16[4,320,128]{2,1,0:T(8,128)(2,1)S(1)}, u32[]{:S(2)}, u32[]{:S(2)}) collective-permute-start(bf16[4,320,128]{2,1,0:T(8,128)(2,1)S(1)} %pad_maximum_fusion.5.refs_0_), channel_id=1, source_target_pairs={{0,8},{4,12},{8,0},{12,4},{1,9},{5,13},{9,1},{13,5},{2,10},{6,14},... | collective-permute-start | bytes 983048 | tf_op jit(solution)/shard_map/ppermute | solution.py:568
  163.6 23.6 %collective-permute-start.68 = (bf16[512,384]{1,0:T(8,128)(2,1)}, bf16[512,384]{1,0:T(8,128)(2,1)S(1)}, u32[]{:S(2)}, u32[]{:S(2)}) collective-permute-start(bf16[512,384]{1,0:T(8,128)(2,1)} %get-tuple-element.134), channel_id=1, source_target_pairs={{0,4},{4,0},{8,12},{12,8},{1,5},{5,1},{9,13},{13,9},{2,6},{6,2},{1... | collective-permute-start | bytes 1179656 | tf_op jit(solution)/shard_map/ppermute | solution.py:568
  169.9 16.7 %collective-permute-start.61 = (bf16[4,320,128]{2,1,0:T(8,128)(2,1)S(1)}, bf16[4,320,128]{2,1,0:T(8,128)(2,1)S(1)}, u32[]{:S(2)}, u32[]{:S(2)}) collective-permute-start(bf16[4,320,128]{2,1,0:T(8,128)(2,1)S(1)} %pad_maximum_fusion.5.refs_0_), channel_id=1, source_target_pairs={{0,16},{16,0},{1,17},{17,1},{2,18},{18,2},{3,19},{19,3},{4,20},{20... | collective-permute-start | bytes 983048 | tf_op jit(solution)/shard_map/ppermute | solution.py:568
  170.5 16.6 %collective-permute-start.53 = (bf16[4,320,128]{2,1,0:T(8,128)(2,1)S(1)}, bf16[4,320,128]{2,1,0:T(8,128)(2,1)S(1)}, u32[]{:S(2)}, u32[]{:S(2)}) collective-permute-start(bf16[4,320,128]{2,1,0:T(8,128)(2,1)S(1)} %collective-permute-done.51.refs_1_), channel_id=1, source_target_pairs={{0,16},{16,0},{1,17},{17,1},{2,18},{18,2},{3,19},{19,3},{4,20},{20... | collective-permute-start | bytes 983048 | tf_op jit(solution)/shard_map/ppermute | solution.py:568
  184.9 12.2 %collective-permute-start.69 = (bf16[512,384]{1,0:T(8,128)(2,1)}, bf16[512,384]{1,0:T(8,128)(2,1)S(1)}, u32[]{:S(2)}, u32[]{:S(2)}) collective-permute-start(bf16[512,384]{1,0:T(8,128)(2,1)} %get-tuple-element.135), channel_id=1, source_target_pairs={{0,8},{4,12},{8,0},{12,4},{1,9},{5,13},{9,1},{13,5},{2,10},{6,14},... | collective-permute-start | bytes 1179656 | tf_op jit(solution)/shard_map/ppermute | solution.py:568
  186.6 23.9 %collective-permute-start.56 = (bf16[4,320,128]{2,1,0:T(8,128)(2,1)S(1)}, bf16[4,320,128]{2,1,0:T(8,128)(2,1)S(1)}, u32[]{:S(2)}, u32[]{:S(2)}) collective-permute-start(bf16[4,320,128]{2,1,0:T(8,128)(2,1)S(1)} %collective-permute-done.52.refs_2_), channel_id=1, source_target_pairs={{0,4},{4,0},{8,12},{12,8},{1,5},{5,1},{9,13},{13,9},{2,6},{6,2},{1... | collective-permute-start | bytes 983048 | tf_op jit(solution)/shard_map/ppermute | solution.py:568
  187.1 25.3 %collective-permute-start.55 = (bf16[4,320,128]{2,1,0:T(8,128)(2,1)S(1)}, bf16[4,320,128]{2,1,0:T(8,128)(2,1)}, u32[]{:S(2)}, u32[]{:S(2)}) collective-permute-start(bf16[4,320,128]{2,1,0:T(8,128)(2,1)S(1)} %collective-permute-done.51.refs_1_), channel_id=1, source_target_pairs={{0,4},{4,0},{8,12},{12,8},{1,5},{5,1},{9,13},{13,9},{2,6},{6,2},{1... | collective-permute-start | bytes 983048 | tf_op jit(solution)/shard_map/ppermute | solution.py:568
  187.2 25.2 %collective-permute-start.63 = (bf16[4,320,128]{2,1,0:T(8,128)(2,1)S(1)}, bf16[4,320,128]{2,1,0:T(8,128)(2,1)S(1)}, u32[]{:S(2)}, u32[]{:S(2)}) collective-permute-start(bf16[4,320,128]{2,1,0:T(8,128)(2,1)S(1)} %collective-permute-done.61.refs_1_), channel_id=1, source_target_pairs={{0,8},{4,12},{8,0},{12,4},{1,9},{5,13},{9,1},{13,5},{2,10},{6,14},... | collective-permute-start | bytes 983048 | tf_op jit(solution)/shard_map/ppermute | solution.py:568
  197.1 16.5 %collective-permute-start.66 = (bf16[4,320,128]{2,1,0:T(8,128)(2,1)S(1)}, bf16[4,320,128]{2,1,0:T(8,128)(2,1)}, u32[]{:S(2)}, u32[]{:S(2)}) collective-permute-start(bf16[4,320,128]{2,1,0:T(8,128)(2,1)S(1)} %collective-permute-done.62.refs_2_), channel_id=1, source_target_pairs={{0,4},{4,0},{8,12},{12,8},{1,5},{5,1},{9,13},{13,9},{2,6},{6,2},{1... | collective-permute-start | bytes 983048 | tf_op jit(solution)/shard_map/ppermute | solution.py:568
  197.1 16.6 %collective-permute-start.57 = (bf16[4,320,128]{2,1,0:T(8,128)(2,1)S(1)}, bf16[4,320,128]{2,1,0:T(8,128)(2,1)}, u32[]{:S(2)}, u32[]{:S(2)}) collective-permute-start(bf16[4,320,128]{2,1,0:T(8,128)(2,1)S(1)} %collective-permute-done.53.refs_3_), channel_id=1, source_target_pairs={{0,4},{4,0},{8,12},{12,8},{1,5},{5,1},{9,13},{13,9},{2,6},{6,2},{1... | collective-permute-start | bytes 983048 | tf_op jit(solution)/shard_map/ppermute | solution.py:568
  213.6 13.1 %collective-permute-start.72 = (bf16[512,128]{1,0:T(8,128)(2,1)}, bf16[512,128]{1,0:T(8,128)(2,1)S(1)}, u32[]{:S(2)}, u32[]{:S(2)}) collective-permute-start(bf16[512,128]{1,0:T(8,128)(2,1)} %get-tuple-element.138), channel_id=1, source_target_pairs={{0,4},{4,0},{8,12},{12,8},{1,5},{5,1},{9,13},{13,9},{2,6},{6,2},{1... | collective-permute-start | bytes 393224 | tf_op jit(solution)/shard_map/ppermute | solution.py:568
  213.7 13.0 %collective-permute-start.73 = (bf16[512,128]{1,0:T(8,128)(2,1)}, bf16[512,128]{1,0:T(8,128)(2,1)S(1)}, u32[]{:S(2)}, u32[]{:S(2)}) collective-permute-start(bf16[512,128]{1,0:T(8,128)(2,1)} %get-tuple-element.139), channel_id=1, source_target_pairs={{0,8},{4,12},{8,0},{12,4},{1,9},{5,13},{9,1},{13,5},{2,10},{6,14},... | collective-permute-start | bytes 393224 | tf_op jit(solution)/shard_map/ppermute | solution.py:568
  260.1 56.9 %collective-permute-start.122 = (bf16[2,8,320,128]{3,2,1,0:T(8,128)(2,1)}, bf16[2,8,320,128]{3,2,1,0:T(8,128)(2,1)S(1)}, u32[]{:S(2)}, u32[]{:S(2)}) collective-permute-start(bf16[2,8,320,128]{3,2,1,0:T(8,128)(2,1)} %get-tuple-element.201), channel_id=1, source_target_pairs={{0,4},{4,0},{8,12},{12,8},{1,5},{5,1},{9,13},{13,9},{2,6},{6,2},{1... | collective-permute-start | bytes 3932168 | tf_op jit(solution)/shard_map/ppermute | solution.py:568
  275.1 12.2 %collective-permute-start.82 = (bf16[512,384]{1,0:T(8,128)(2,1)}, bf16[512,384]{1,0:T(8,128)(2,1)S(1)}, u32[]{:S(2)}, u32[]{:S(2)}) collective-permute-start(bf16[512,384]{1,0:T(8,128)(2,1)} %get-tuple-element.157), channel_id=1, source_target_pairs={{0,8},{4,12},{8,0},{12,4},{1,9},{5,13},{9,1},{13,5},{2,10},{6,14},... | collective-permute-start | bytes 1179656 | tf_op jit(solution)/shard_map/ppermute | solution.py:568
  282.5 38.1 %collective-permute-start.110 = (bf16[2,8,320,128]{3,2,1,0:T(8,128)(2,1)}, bf16[2,8,320,128]{3,2,1,0:T(8,128)(2,1)S(1)}, u32[]{:S(2)}, u32[]{:S(2)}) collective-permute-start(bf16[2,8,320,128]{3,2,1,0:T(8,128)(2,1)} %get-tuple-element.195), channel_id=1, source_target_pairs={{0,4},{4,0},{8,12},{12,8},{1,5},{5,1},{9,13},{13,9},{2,6},{6,2},{1... | collective-permute-start | bytes 3932168 | tf_op jit(solution)/shard_map/ppermute | solution.py:568
  318.3 36.9 %collective-permute-start.123 = (bf16[2,4,320,128]{3,2,1,0:T(8,128)(2,1)}, bf16[2,4,320,128]{3,2,1,0:T(8,128)(2,1)S(1)}, u32[]{:S(2)}, u32[]{:S(2)}) collective-permute-start(bf16[2,4,320,128]{3,2,1,0:T(8,128)(2,1)} %bitcast.146), channel_id=1, source_target_pairs={{0,8},{4,12},{8,0},{12,4},{1,9},{5,13},{9,1},{13,5},{2,10},{6,14},... | collective-permute-start | bytes 1966088 | tf_op jit(solution)/shard_map/ppermute | solution.py:568
  335.1 14.9 %collective-permute-start.89 = (bf16[512,384]{1,0:T(8,128)(2,1)}, bf16[512,384]{1,0:T(8,128)(2,1)}, u32[]{:S(2)}, u32[]{:S(2)}) collective-permute-start(bf16[512,384]{1,0:T(8,128)(2,1)} %get-tuple-element.173), channel_id=1, source_target_pairs={{0,8},{4,12},{8,0},{12,4},{1,9},{5,13},{9,1},{13,5},{2,10},{6,14},... | collective-permute-start | bytes 1179656 | tf_op jit(solution)/shard_map/ppermute | solution.py:568
  336.7 19.2 %collective-permute-start.111 = (bf16[2,4,320,128]{3,2,1,0:T(8,128)(2,1)}, bf16[2,4,320,128]{3,2,1,0:T(8,128)(2,1)S(1)}, u32[]{:S(2)}, u32[]{:S(2)}) collective-permute-start(bf16[2,4,320,128]{3,2,1,0:T(8,128)(2,1)} %get-tuple-element.209), channel_id=1, source_target_pairs={{0,16},{16,0},{1,17},{17,1},{2,18},{18,2},{3,19},{19,3},{4,20},{20... | collective-permute-start | bytes 1966088 | tf_op jit(solution)/shard_map/ppermute | solution.py:568
  337.5 17.6 %collective-permute-start.90 = (bf16[512,384]{1,0:T(8,128)(2,1)}, bf16[512,384]{1,0:T(8,128)(2,1)}, u32[]{:S(2)}, u32[]{:S(2)}) collective-permute-start(bf16[512,384]{1,0:T(8,128)(2,1)} %get-tuple-element.174), channel_id=1, source_target_pairs={{0,8},{4,12},{8,0},{12,4},{1,9},{5,13},{9,1},{13,5},{2,10},{6,14},... | collective-permute-start | bytes 1179656 | tf_op jit(solution)/shard_map/ppermute | solution.py:568
  344.7 27.0 %collective-permute-start.104 = (bf16[2,8,320,128]{3,2,1,0:T(8,128)(2,1)}, bf16[2,8,320,128]{3,2,1,0:T(8,128)(2,1)S(1)}, u32[]{:S(2)}, u32[]{:S(2)}) collective-permute-start(bf16[2,8,320,128]{3,2,1,0:T(8,128)(2,1)} %get-tuple-element.189), channel_id=1, source_target_pairs={{0,4},{4,0},{8,12},{12,8},{1,5},{5,1},{9,13},{13,9},{2,6},{6,2},{1... | collective-permute-start | bytes 3932168 | tf_op jit(solution)/shard_map/ppermute | solution.py:568
  350.0 23.8 %collective-permute-start.116 = (bf16[2,8,320,128]{3,2,1,0:T(8,128)(2,1)}, bf16[2,8,320,128]{3,2,1,0:T(8,128)(2,1)S(1)}, u32[]{:S(2)}, u32[]{:S(2)}) collective-permute-start(bf16[2,8,320,128]{3,2,1,0:T(8,128)(2,1)} %get-tuple-element.198), channel_id=1, source_target_pairs={{0,4},{4,0},{8,12},{12,8},{1,5},{5,1},{9,13},{13,9},{2,6},{6,2},{1... | collective-permute-start | bytes 3932168 | tf_op jit(solution)/shard_map/ppermute | solution.py:568
  355.2 22.9 %collective-permute-start.98 = (bf16[2,8,320,128]{3,2,1,0:T(8,128)(2,1)}, bf16[2,8,320,128]{3,2,1,0:T(8,128)(2,1)}, u32[]{:S(2)}, u32[]{:S(2)}) collective-permute-start(bf16[2,8,320,128]{3,2,1,0:T(8,128)(2,1)} %get-tuple-element.183), channel_id=1, source_target_pairs={{0,4},{4,0},{8,12},{12,8},{1,5},{5,1},{9,13},{13,9},{2,6},{6,2},{1... | collective-permute-start | bytes 3932168 | tf_op jit(solution)/shard_map/ppermute | solution.py:568
  355.9 14.5 %collective-permute-start.124 = (bf16[4,320,128]{2,1,0:T(8,128)(2,1)S(1)}, bf16[4,320,128]{2,1,0:T(8,128)(2,1)S(1)}, u32[]{:S(2)}, u32[]{:S(2)}) collective-permute-start(bf16[4,320,128]{2,1,0:T(8,128)(2,1)S(1)} %get-tuple-element.217), channel_id=1, source_target_pairs={{0,16},{16,0},{1,17},{17,1},{2,18},{18,2},{3,19},{19,3},{4,20},{20... | collective-permute-start | bytes 983048 | tf_op jit(solution)/shard_map/ppermute | solution.py:568
  358.6 12.2 %collective-permute-start.112 = (bf16[4,320,128]{2,1,0:T(8,128)(2,1)S(1)}, bf16[4,320,128]{2,1,0:T(8,128)(2,1)S(1)}, u32[]{:S(2)}, u32[]{:S(2)}) collective-permute-start(bf16[4,320,128]{2,1,0:T(8,128)(2,1)S(1)} %get-tuple-element.221), channel_id=1, source_target_pairs={{0,8},{4,12},{8,0},{12,4},{1,9},{5,13},{9,1},{13,5},{2,10},{6,14},... | collective-permute-start | bytes 983048 | tf_op jit(solution)/shard_map/ppermute | solution.py:568
  370.4 56.4 %collective-permute-start.92 = (bf16[2,8,320,128]{3,2,1,0:T(8,128)(2,1)}, bf16[2,8,320,128]{3,2,1,0:T(8,128)(2,1)S(1)}, u32[]{:S(2)}, u32[]{:S(2)}) collective-permute-start(bf16[2,8,320,128]{3,2,1,0:T(8,128)(2,1)} %get-tuple-element.179), channel_id=1, source_target_pairs={{0,4},{4,0},{8,12},{12,8},{1,5},{5,1},{9,13},{13,9},{2,6},{6,2},{1... | collective-permute-start | bytes 3932168 | tf_op jit(solution)/shard_map/ppermute | solution.py:568
  371.7 13.0 %collective-permute-start.127 = (bf16[320,128]{1,0:T(8,128)(2,1)S(1)}, bf16[320,128]{1,0:T(8,128)(2,1)S(1)}, u32[]{:S(2)}, u32[]{:S(2)}) collective-permute-start(bf16[320,128]{1,0:T(8,128)(2,1)S(1)} %get-tuple-element.230), channel_id=1, source_target_pairs={{0,3},{1,2},{2,1},{3,0},{4,7},{5,6},{6,5},{7,4},{8,11},{9,10},{10,... | collective-permute-start | bytes 245768 | tf_op jit(solution)/shard_map/ppermute | solution.py:568
  385.5 18.0 %collective-permute-start.117 = (bf16[2,4,320,128]{3,2,1,0:T(8,128)(2,1)}, bf16[2,4,320,128]{3,2,1,0:T(8,128)(2,1)}, u32[]{:S(2)}, u32[]{:S(2)}) collective-permute-start(bf16[2,4,320,128]{3,2,1,0:T(8,128)(2,1)} %bitcast.133), channel_id=1, source_target_pairs={{0,8},{4,12},{8,0},{12,4},{1,9},{5,13},{9,1},{13,5},{2,10},{6,14},... | collective-permute-start | bytes 1966088 | tf_op jit(solution)/shard_map/ppermute | solution.py:568
  389.8 17.9 %collective-permute-start.105 = (bf16[2,4,320,128]{3,2,1,0:T(8,128)(2,1)}, bf16[2,4,320,128]{3,2,1,0:T(8,128)(2,1)S(1)}, u32[]{:S(2)}, u32[]{:S(2)}) collective-permute-start(bf16[2,4,320,128]{3,2,1,0:T(8,128)(2,1)} %get-tuple-element.207), channel_id=1, source_target_pairs={{0,16},{16,0},{1,17},{17,1},{2,18},{18,2},{3,19},{19,3},{4,20},{20... | collective-permute-start | bytes 1966088 | tf_op jit(solution)/shard_map/ppermute | solution.py:568
  390.9 26.5 %collective-permute-start.99 = (bf16[2,4,320,128]{3,2,1,0:T(8,128)(2,1)}, bf16[2,4,320,128]{3,2,1,0:T(8,128)(2,1)S(1)}, u32[]{:S(2)}, u32[]{:S(2)}) collective-permute-start(bf16[2,4,320,128]{3,2,1,0:T(8,128)(2,1)} %bitcast.421), channel_id=1, source_target_pairs={{0,8},{4,12},{8,0},{12,4},{1,9},{5,13},{9,1},{13,5},{2,10},{6,14},... | collective-permute-start | bytes 1966088 | tf_op jit(solution)/shard_map/ppermute | solution.py:568
  404.7 14.0 %collective-permute-start.118 = (bf16[4,320,128]{2,1,0:T(8,128)(2,1)S(1)}, bf16[4,320,128]{2,1,0:T(8,128)(2,1)S(1)}, u32[]{:S(2)}, u32[]{:S(2)}) collective-permute-start(bf16[4,320,128]{2,1,0:T(8,128)(2,1)S(1)} %get-tuple-element.215), channel_id=1, source_target_pairs={{0,16},{16,0},{1,17},{17,1},{2,18},{18,2},{3,19},{19,3},{4,20},{20... | collective-permute-start | bytes 983048 | tf_op jit(solution)/shard_map/ppermute | solution.py:568
  407.9 14.8 %collective-permute-start.106 = (bf16[4,320,128]{2,1,0:T(8,128)(2,1)S(1)}, bf16[4,320,128]{2,1,0:T(8,128)(2,1)S(1)}, u32[]{:S(2)}, u32[]{:S(2)}) collective-permute-start(bf16[4,320,128]{2,1,0:T(8,128)(2,1)S(1)} %get-tuple-element.219), channel_id=1, source_target_pairs={{0,8},{4,12},{8,0},{12,4},{1,9},{5,13},{9,1},{13,5},{2,10},{6,14},... | collective-permute-start | bytes 983048 | tf_op jit(solution)/shard_map/ppermute | solution.py:568
  425.2 17.6 %collective-permute-start.107 = (bf16[320,128]{1,0:T(8,128)(2,1)}, bf16[320,128]{1,0:T(8,128)(2,1)S(1)}, u32[]{:S(2)}, u32[]{:S(2)}) collective-permute-start(bf16[320,128]{1,0:T(8,128)(2,1)} %get-tuple-element.232), channel_id=1, source_target_pairs={{0,1},{1,0},{2,3},{3,2},{4,5},{5,4},{6,7},{7,6},{8,9},{9,8},{10,11... | collective-permute-start | bytes 245768 | tf_op jit(solution)/shard_map/ppermute | solution.py:568
  426.8 16.0 %collective-permute-start.109 = (bf16[320,128]{1,0:T(8,128)(2,1)}, bf16[320,128]{1,0:T(8,128)(2,1)}, u32[]{:S(2)}, u32[]{:S(2)}) collective-permute-start(bf16[320,128]{1,0:T(8,128)(2,1)} %get-tuple-element.233), channel_id=1, source_target_pairs={{0,3},{1,2},{2,1},{3,0},{4,7},{5,6},{6,5},{7,4},{8,11},{9,10},{10,... | collective-permute-start | bytes 245768 | tf_op jit(solution)/shard_map/ppermute | solution.py:568
  436.7 12.4 %collective-permute-start.93 = (bf16[2,4,320,128]{3,2,1,0:T(8,128)(2,1)S(1)}, bf16[2,4,320,128]{3,2,1,0:T(8,128)(2,1)S(1)}, u32[]{:S(2)}, u32[]{:S(2)}) collective-permute-start(bf16[2,4,320,128]{3,2,1,0:T(8,128)(2,1)S(1)} %bitcast.420), channel_id=1, source_target_pairs={{0,8},{4,12},{8,0},{12,4},{1,9},{5,13},{9,1},{13,5},{2,10},{6,14},... | collective-permute-start | bytes 1966088 | tf_op jit(solution)/shard_map/ppermute | solution.py:568
  (153 other events, 1676.7 us)
